TPU v7x, 128 devices: a whole 4x4x4 slice. The times are simulated.
128 devices in a mesh: dp: 16 (over y, x_hi, core), tensor: 8 (over x_lo, z).
Axes of the slice: x: 4 (x_hi: 2, x_lo: 2; x = x_hi * 2 + x_lo), y: 4, z: 4, core: 2. Of those that a mesh axis runs over, the one named last changes fastest.
Arguments:
- token_ids: int32 [1024, 4], P('dp'), may hold values from 0 to 76799
- lengths: int32 [1024], P('dp'), may hold values from 1 to 512, as said below
- embed_table: bfloat16 [76800, 5120], P('dp', 'tensor'), may hold values from -6 to 6
- norm_gain: bfloat16 [5120], P('tensor'), may hold values from 0.099609375 to 1.8984375
- w_query: bfloat16 [5120, 8192], P(('dp', 'tensor')), may hold values from -0.078125 to 0.078125
- w_key: bfloat16 [5120, 1024], P(('dp', 'tensor')), may hold values from -0.078125 to 0.078125
- w_value: bfloat16 [5120, 1024], P(('dp', 'tensor')), may hold values from -0.078125 to 0.078125
- w_out: bfloat16 [8192, 5120], P(('dp', 'tensor')), may hold values from -0.0625 to 0.0625
- q_gain: bfloat16 [128], replicated, may hold values from 0.099609375 to 1.8984375
- k_gain: bfloat16 [128], replicated, may hold values from 0.099609375 to 1.8984375
- key_cache: bfloat16 [1024, 512, 1024], P('dp', None, 'tensor'), may hold values from -160 to 160
- value_cache: bfloat16 [1024, 512, 1024], P('dp', None, 'tensor'), may hold values from -6 to 6
Outputs:
- attended: bfloat16 [1024, 4, 5120], P('dp', None, 'tensor')
- new_keys: bfloat16 [1024, 4, 1024], P('dp', None, 'tensor')
- new_values: bfloat16 [1024, 4, 1024], P('dp', None, 'tensor')
Inputs may be any that keep to these rules, and one draw needn't show every extreme that they name: `lengths`: at least one row holds 512 cached positions.
All inputs are finite; a program needn't handle non-finite values.
Results may differ from a plain program's by a relative error of at most 0.0066.
Values may be sent and summed in bfloat16 or wider, within the bound.
A program may use at most 192 MiB of HBM per device.

v0:
```python
import math

import jax
import jax.numpy as jnp
from jax import lax
from jax.sharding import PartitionSpec as P

EPS = 1e-06
THETA = 1000000.0


def rms_scale(values, gain):
    mean_sq = jnp.mean(values * values, axis=-1, keepdims=True)
    return values * lax.rsqrt(mean_sq + EPS) * gain.astype(jnp.float32)


def rotate(values, positions):
    half = values.shape[-1] // 2
    freq = THETA ** (-jnp.arange(half, dtype=jnp.float32) * 2.0 / values.shape[-1])
    angle = positions.astype(jnp.float32)[:, :, None, None] * freq
    cosine = jnp.cos(angle)
    sine = jnp.sin(angle)
    first = values[..., :half]
    second = values[..., half:]
    return jnp.concatenate(
        [first * cosine - second * sine, second * cosine + first * sine], axis=-1
    )


def attend(query, fresh_keys, fresh_values, key_cache, value_cache, lengths):
    rows, steps, heads_count, width = query.shape
    kv_heads = fresh_keys.shape[2]
    group = heads_count // kv_heads
    cache_len = key_cache.shape[1]
    grouped = query.reshape(rows, steps, kv_heads, group, width)
    keys = key_cache.reshape(rows, cache_len, kv_heads, width)
    values = value_cache.reshape(rows, cache_len, kv_heads, width)
    scale = 1.0 / math.sqrt(width)
    old_scores = (
        jnp.einsum("rskgd,rckd->rkgsc", grouped, keys, preferred_element_type=jnp.float32) * scale
    )
    new_scores = (
        jnp.einsum("rskgd,rtkd->rkgst", grouped, fresh_keys, preferred_element_type=jnp.float32)
        * scale
    )
    valid = jnp.arange(cache_len)[None, :] < lengths[:, None]
    old_scores = jnp.where(valid[:, None, None, None, :], old_scores, -jnp.inf)
    causal = jnp.arange(steps)[None, :] <= jnp.arange(steps)[:, None]
    new_scores = jnp.where(causal[None, None, None, :, :], new_scores, -jnp.inf)
    highest = jnp.maximum(jnp.max(old_scores, axis=-1), jnp.max(new_scores, axis=-1))
    old_exp = jnp.exp(old_scores - highest[..., None])
    new_exp = jnp.exp(new_scores - highest[..., None])
    total = jnp.sum(old_exp, axis=-1) + jnp.sum(new_exp, axis=-1)
    old_weights = (old_exp / total[..., None]).astype(jnp.bfloat16)
    new_weights = (new_exp / total[..., None]).astype(jnp.bfloat16)
    mixed = jnp.einsum("rkgsc,rckd->rskgd", old_weights, values, preferred_element_type=jnp.float32)
    mixed = mixed + jnp.einsum(
        "rkgst,rtkd->rskgd", new_weights, fresh_values, preferred_element_type=jnp.float32
    )
    return mixed.reshape(rows, steps, heads_count * width).astype(jnp.bfloat16)


def spread(local, replicas, owners):
    height, breadth = local.shape
    blocks = local.reshape(height, 1, owners, breadth // owners)
    tiled = jnp.broadcast_to(blocks, (height, replicas, owners, breadth // owners))
    return tiled.reshape(height, replicas * breadth)


def shards(
    token_ids,
    lengths,
    embed_table,
    norm_gain,
    w_query,
    w_key,
    w_value,
    w_out,
    q_gain,
    k_gain,
    key_cache,
    value_cache,
):
    replicas = lax.axis_size("dp")
    owners = lax.axis_size("tensor")
    rows, steps = token_ids.shape
    width = q_gain.shape[0]
    every_id = lax.all_gather(token_ids, "dp", axis=0, tiled=True)
    vocab_rows = embed_table.shape[0]
    local_id = every_id - lax.axis_index("dp") * vocab_rows
    inside = (local_id >= 0) & (local_id < vocab_rows)
    picked = jnp.take(embed_table, jnp.clip(local_id, 0, vocab_rows - 1), axis=0)
    partial_rows = jnp.where(inside[..., None], picked, jnp.zeros((), jnp.bfloat16))
    own_rows = lax.psum_scatter(
        partial_rows.astype(jnp.float32).astype(jnp.bfloat16), "dp", scatter_dimension=0, tiled=True
    )
    whole, gain_full = (
        lax.all_gather(own_rows, "tensor", axis=2, tiled=True),
        lax.all_gather(norm_gain, "tensor", axis=0, tiled=True),
    )
    normed = rms_scale(whole.astype(jnp.float32), gain_full).astype(jnp.bfloat16)
    flat = normed.reshape(rows * steps, -1)
    pieces = (
        lax.all_to_all(
            spread(w_query, replicas, owners),
            ("dp", "tensor"),
            split_axis=1,
            concat_axis=0,
            tiled=True,
        ),
        lax.all_to_all(
            spread(w_key, replicas, owners),
            ("dp", "tensor"),
            split_axis=1,
            concat_axis=0,
            tiled=True,
        ),
        lax.all_to_all(
            spread(w_value, replicas, owners),
            ("dp", "tensor"),
            split_axis=1,
            concat_axis=0,
            tiled=True,
        ),
        lax.all_to_all(
            spread(w_out, replicas, owners),
            ("dp", "tensor"),
            split_axis=1,
            concat_axis=0,
            tiled=True,
        ),
    )
    query_raw = jnp.dot(flat, pieces[0], preferred_element_type=jnp.float32)
    key_raw = jnp.dot(flat, pieces[1], preferred_element_type=jnp.float32)
    value_raw = jnp.dot(flat, pieces[2], preferred_element_type=jnp.float32)
    out_local = pieces[3]
    positions = lengths[:, None] + jnp.arange(steps, dtype=jnp.int32)[None, :]
    query_raw = query_raw.reshape(rows, steps, -1, width)
    key_raw = key_raw.reshape(rows, steps, -1, width)
    fresh_values = value_raw.astype(jnp.bfloat16).reshape(rows, steps, -1, width)
    query = rotate(rms_scale(query_raw, q_gain), positions).astype(jnp.bfloat16)
    fresh_keys = rotate(rms_scale(key_raw, k_gain), positions).astype(jnp.bfloat16)
    local_heads = attend(query, fresh_keys, fresh_values, key_cache, value_cache, lengths)
    all_heads = lax.all_gather(local_heads, "tensor", axis=2, tiled=True).reshape(rows * steps, -1)
    projected = jnp.dot(all_heads, out_local, preferred_element_type=jnp.float32)
    output = projected + own_rows.astype(jnp.float32).reshape(rows * steps, -1)
    attended = output.astype(jnp.bfloat16).reshape(rows, steps, -1)
    return (attended, fresh_keys.reshape(rows, steps, -1), fresh_values.reshape(rows, steps, -1))


def solution(mesh):
    in_specs = (
        P("dp", None),
        P("dp"),
        P("dp", "tensor"),
        P("tensor"),
        P(("dp", "tensor"), None),
        P(("dp", "tensor"), None),
        P(("dp", "tensor"), None),
        P(("dp", "tensor"), None),
        P(),
        P(),
        P("dp", None, "tensor"),
        P("dp", None, "tensor"),
    )
    out_specs = (P("dp", None, "tensor"), P("dp", None, "tensor"), P("dp", None, "tensor"))
    return jax.shard_map(shards, mesh=mesh, in_specs=in_specs, out_specs=out_specs, check_vma=False)
```

profile of v0, /device:TPU:1, one launch (start us, length us, event | category | flops | bytes accessed | tf_op | source)
XLA Modules:
  0.0 638.3 jit_solution(2010330971087645914)
XLA Ops:
  7.2 26.1 %all-gather = s32[16,64,4]{1,2,0:T(4,128)S(1)} all-gather(s32[1,64,4]{1,2,0:T(4,128)} %bitcast.157), channel_id=1, replica_groups=mesh['dp'=16,'tensor'=8] {'dp'}, dimensions={0}, use_global_device_ids=true | all-gather | bytes 17408 | tf_op jit(solution)/shard_map/all_gather | solution.py:88
  34.0 21.5 %gather_fusion = bf16[4096,640]{1,0:T(8,128)(2,1)} fusion(bf16[4800,640]{1,0:T(8,128)(2,1)} %param.14, s32[4096]{0:T(1024)S(1)} %broadcast_clamp_fusion), kind=kCustom, calls=%fused_computation | custom fusion | bytes 10502144 | tf_op jit(solution)/shard_map/jit(_take)/gather | solution.py:92
  55.5 9.5 %reshape.302 = bf16[1024,4,640]{2,1,0:T(4,128)(2,1)} reshape(bf16[4096,640]{1,0:T(8,128)(2,1)} %gather_fusion) | data formatting | bytes 10485760 | tf_op jit(solution)/shard_map/jit(_take)/gather | solution.py:92
  65.6 10.5 %select_select_fusion = bf16[1024,4,640]{2,1,0:T(4,128)(2,1)} fusion(bf16[1024,4,640]{2,1,0:T(4,128)(2,1)} %reshape.302, pred[1024,4]{1,0:T(8,128)(4,1)S(1)} %copy.65, pred[1024,4]{1,0:T(8,128)(4,1)S(1)} %bitcast.151), kind=kLoop, calls=%fused_computation.10 | loop fusion | flops 5242880 | bytes 10493952 | tf_op jit(solution)/shard_map/jit(_where)/select_n | solution.py:93
  77.6 5.1 all-to-all-start.1
  82.7 35.2 %all-to-all-done.1 = bf16[40,128,128]{2,0,1:T(8,128)(2,1)S(1)} async-done(((bf16[40,128,128]{2,0,1:T(8,128)(2,1)}), bf16[40,128,128]{2,0,1:T(8,128)(2,1)S(1)}, u32[]{:S(2)}, u32[]{:S(2)}) %all-to-all-start.1) | async-done | bytes 1310752 | tf_op jit(solution)/shard_map/all_to_all | solution.py:111
  119.4 5.6 all-to-all-start.2
  125.1 34.2 %all-to-all-done.2 = bf16[40,128,128]{2,0,1:T(8,128)(2,1)S(1)} async-done(((bf16[40,128,128]{2,0,1:T(8,128)(2,1)}), bf16[40,128,128]{2,0,1:T(8,128)(2,1)S(1)}, u32[]{:S(2)}, u32[]{:S(2)}) %all-to-all-start.2) | async-done | bytes 1310752 | tf_op jit(solution)/shard_map/all_to_all | solution.py:118
  159.3 5.2 broadcast_in_dim.106
  164.5 10.5 %all-to-all-start = ((bf16[40,128,1024]{2,0,1:T(8,128)(2,1)}), bf16[40,128,1024]{2,0,1:T(8,128)(2,1)}, u32[]{:S(2)}, u32[]{:S(2)}) async-start(bf16[40,128,1024]{2,0,1:T(8,128)(2,1)} %bitcast.140), calls=%async_computation | async-start | bytes 20971520 | tf_op jit(solution)/shard_map/all_to_all | solution.py:104
  176.3 118.3 %all-reduce.3.cloned.1.call-done = bf16[1024,4,640]{2,1,0:T(4,128)(2,1)} async-done(((bf16[1024,4,640]{2,1,0:T(4,128)(2,1)}), bf16[1024,4,640]{2,1,0:T(4,128)(2,1)}) %all-reduce.3.cloned.1.call-update) | async-done | bytes 5242896
  296.4 97.5 %all-gather.1 = bf16[8,1,640]{2,1,0:T(2,128)(2,1)S(1)} all-gather(bf16[1,1,640]{2,1,0:T(2,128)(2,1)S(1)} %reshape.313), channel_id=1, replica_groups=mesh['dp'=16,'tensor'=8] {'tensor'}, dimensions={0}, use_global_device_ids=true | all-gather | bytes 11520 | tf_op jit(solution)/shard_map/all_gather | solution.py:99
  396.1 3.3 fusion.4
  399.5 3.1 fusion.6
  402.5 5.2 reshape.290
  407.8 3.0 multiply_reduce_fusion.1
  416.1 3.0 fusion.55
  419.1 5.5 broadcast_in_dim.115
  424.6 17.3 %all-to-all-start.3 = ((bf16[64,128,640]{2,0,1:T(8,128)(2,1)}), bf16[64,128,640]{2,0,1:T(8,128)(2,1)}, u32[]{:S(2)}, u32[]{:S(2)}) async-start(bf16[64,128,640]{2,0,1:T(8,128)(2,1)} %bitcast.141), calls=%async_computation.3 | async-start | bytes 20971520 | tf_op jit(solution)/shard_map/all_to_all | solution.py:125
  442.3 14.0 %copy.70 = bf16[1024,5120]{1,0:T(8,128)(2,1)} copy(bf16[1024,5120]{0,1:T(8,128)(2,1)} %bitcast.7) | data formatting | bytes 20971520 | tf_op jit(solution)/shard_map/dot_general | solution.py:133
  456.3 6.1 multiply_reduce_fusion
  475.0 140.4 %all-gather.7.cloned.1.call-done = bf16[64,4,8192]{2,1,0:T(4,128)(2,1)} async-done(((bf16[64,4,1024]{2,1,0:T(4,128)(2,1)}), bf16[64,4,8192]{2,1,0:T(4,128)(2,1)}) %all-gather.7.cloned.1.call-update) | async-done | bytes 4194320 | tf_op jit(solution)/shard_map/all_gather | solution.py:144
  615.4 6.9 %reshape.295 = bf16[256,8192]{1,0:T(8,128)(2,1)} reshape(bf16[64,4,8192]{2,1,0:T(4,128)(2,1)} %all-gather.7.cloned.1.call-done) | data formatting | bytes 8388608 | tf_op jit(solution)/shard_map/reshape | solution.py:144
  622.3 8.7 %fusion.25 = bf16[256,640]{1,0:T(8,128)(2,1)S(1)} fusion(f32[256,640]{1,0:T(8,128)S(1)} %reshape.300, bf16[256,8192]{1,0:T(8,128)(2,1)} %reshape.295, bf16[8192,640]{1,0:T(8,128)(2,1)} %bitcast.40), kind=kOutput, calls=%fused_computation.31 | convolution fusion | flops 2684682240 | bytes 15663104 | tf_op jit(solution)/shard_map/dot_general | solution.py:145
  (107 shorter events, 27.6 us)
Async XLA Ops:
  7.2 69.0 %copy-start = (bf16[40,1024]{1,0:T(8,128)(2,1)S(1)}, bf16[40,1024]{1,0:T(8,128)(2,1)}, u32[]{:S(2)}) copy-start(bf16[40,1024]{1,0:T(8,128)(2,1)} %param.17) | copy-start | bytes 245764
  7.2 287.4 %all-reduce.3.cloned.1.call-start = ((), (), s32[]{:S(2)}) async-start(), calls=%async_computation.6 | async-start | bytes 10485760
  76.2 6.5 %copy-start.11 = (bf16[40,1024]{1,0:T(8,128)(2,1)S(1)}, bf16[40,1024]{1,0:T(8,128)(2,1)}, u32[]{:S(2)}) copy-start(bf16[40,1024]{1,0:T(8,128)(2,1)} %param.18) | copy-start | bytes 245764
  76.2 48.9 %copy-start.7 = (bf16[40,8192]{1,0:T(8,128)(2,1)S(1)}, bf16[40,8192]{1,0:T(8,128)(2,1)}, u32[]{:S(2)}) copy-start(bf16[40,8192]{1,0:T(8,128)(2,1)} %param.16) | copy-start | bytes 1966084
  77.6 40.3 %all-to-all-start.1 = ((bf16[40,128,128]{2,0,1:T(8,128)(2,1)}), bf16[40,128,128]{2,0,1:T(8,128)(2,1)S(1)}, u32[]{:S(2)}, u32[]{:S(2)}) async-start(bf16[40,128,128]{2,0,1:T(8,128)(2,1)} %bitcast.15), calls=%async_computation.1 | async-start | bytes 2621440 | tf_op jit(solution)/shard_map/all_to_all | solution.py:111
  119.4 39.9 %all-to-all-start.2 = ((bf16[40,128,128]{2,0,1:T(8,128)(2,1)}), bf16[40,128,128]{2,0,1:T(8,128)(2,1)S(1)}, u32[]{:S(2)}, u32[]{:S(2)}) async-start(bf16[40,128,128]{2,0,1:T(8,128)(2,1)} %bitcast.29), calls=%async_computation.2 | async-start | bytes 2621440 | tf_op jit(solution)/shard_map/all_to_all | solution.py:118
  164.5 10.6 %copy-start.18 = (u32[128]{0:T(128)S(1)}, u32[128]{0:T(128)}, u32[]{:S(2)}) copy-start(u32[128]{0:T(128)} %constant.61) | copy-start | bytes 1540
  164.5 131.9 %copy-start.15 = (bf16[640]{0:T(1024)(128)(2,1)S(1)}, bf16[640]{0:T(1024)(128)(2,1)}, u32[]{:S(2)}) copy-start(bf16[640]{0:T(1024)(128)(2,1)} %param.15) | copy-start | bytes 3844
  164.5 229.4 %copy-start.16 = (bf16[128]{0:T(256)(128)(2,1)S(1)}, bf16[128]{0:T(256)(128)(2,1)}, u32[]{:S(2)}) copy-start(bf16[128]{0:T(256)(128)(2,1)} %param.20) | copy-start | bytes 772
  164.5 229.4 %copy-start.17 = (bf16[128]{0:T(256)(128)(2,1)S(1)}, bf16[128]{0:T(256)(128)(2,1)}, u32[]{:S(2)}) copy-start(bf16[128]{0:T(256)(128)(2,1)} %param.21) | copy-start | bytes 772
  164.5 229.4 %copy-start.14 = (s32[64]{0:T(128)S(1)}, s32[64]{0:T(128)}, u32[]{:S(2)}) copy-start(s32[64]{0:T(128)} %param.13) | copy-start | bytes 772
  164.5 230.1 %copy-start.8 = (bf16[64,5120]{1,0:T(8,128)(2,1)S(1)}, bf16[64,5120]{1,0:T(8,128)(2,1)}, u32[]{:S(2)}) copy-start(bf16[64,5120]{1,0:T(8,128)(2,1)} %param.19) | copy-start | bytes 1966084
  164.5 254.6 %all-to-all-start = ((bf16[40,128,1024]{2,0,1:T(8,128)(2,1)}), bf16[40,128,1024]{2,0,1:T(8,128)(2,1)}, u32[]{:S(2)}, u32[]{:S(2)}) async-start(bf16[40,128,1024]{2,0,1:T(8,128)(2,1)} %bitcast.140), calls=%async_computation | async-start | bytes 20971520 | tf_op jit(solution)/shard_map/all_to_all | solution.py:104
  175.0 221.1 %all-gather.5.cloned.1.call-start = ((), (), s32[]{:S(2)}) async-start(), calls=%async_computation.4 | async-start | bytes 2949120 | tf_op jit(solution)/shard_map/all_gather | solution.py:98
  413.1 50.5 %copy-start.13 = (bf16[64,4,128]{2,1,0:T(4,128)(2,1)}, bf16[64,4,128]{2,1,0:T(4,128)(2,1)S(1)}, u32[]{:S(2)}) copy-start(bf16[64,4,128]{2,1,0:T(4,128)(2,1)S(1)} %pad_maximum_fusion.1) | copy-start | bytes 196612
  416.1 57.3 %copy-start.12 = (bf16[256,128]{1,0:T(8,128)(2,1)}, bf16[256,128]{1,0:T(8,128)(2,1)S(1)}, u32[]{:S(2)}) copy-start(bf16[256,128]{1,0:T(8,128)(2,1)S(1)} %convolution_convert_fusion) | copy-start | bytes 196612
  424.6 197.6 %all-to-all-start.3 = ((bf16[64,128,640]{2,0,1:T(8,128)(2,1)}), bf16[64,128,640]{2,0,1:T(8,128)(2,1)}, u32[]{:S(2)}, u32[]{:S(2)}) async-start(bf16[64,128,640]{2,0,1:T(8,128)(2,1)} %bitcast.141), calls=%async_computation.3 | async-start | bytes 20971520 | tf_op jit(solution)/shard_map/all_to_all | solution.py:125
  442.0 173.4 %all-gather.7.cloned.1.call-start = ((), (), s32[]{:S(2)}) async-start(), calls=%async_computation.5 | async-start | bytes 4718592 | tf_op jit(solution)/shard_map/all_gather | solution.py:144
  442.3 14.0 %copy-start.6 = (bf16[64,4,5120,1]{2,1,0,3:T(4,128)(2,1)S(1)}, bf16[64,4,5120,1]{2,1,0,3:T(4,128)(2,1)}, u32[]{:S(2)}) copy-start(bf16[64,4,5120,1]{2,1,0,3:T(4,128)(2,1)} %fusion.55) | copy-start | bytes 7864324
  456.3 9.9 %slice-start = ((s8[8388608]{0:T(1024)(128)(4,1)}), s8[4194304]{0:T(1024)(128)(4,1)S(1)}, s32[]{:S(2)}) async-start(s8[8388608]{0:T(1024)(128)(4,1)} %bitcast.143), calls=%async_computation.7 | async-start | bytes 8388608
  456.3 6.5 %copy-start.10 = (f32[64,4,64]{2,0,1:T(8,128)S(1)}, f32[64,4,64]{2,0,1:T(8,128)}, u32[]{:S(2)}) copy-start(f32[64,4,64]{2,0,1:T(8,128)} %get-tuple-element.8) | copy-start | bytes 196612
  456.3 9.9 %slice-start.1 = ((s8[8388608]{0:T(1024)(128)(4,1)}), s8[4194304]{0:T(1024)(128)(4,1)S(1)}, s32[]{:S(2)}) async-start(s8[8388608]{0:T(1024)(128)(4,1)} %bitcast.143), calls=%async_computation.8 | async-start | bytes 8388608
  463.6 7.9 %slice-start.2 = ((s8[8388608]{0:T(1024)(128)(4,1)}), s8[4194304]{0:T(1024)(128)(4,1)S(1)}, s32[]{:S(2)}) async-start(s8[8388608]{0:T(1024)(128)(4,1)} %bitcast.158), calls=%async_computation.9 | async-start | bytes 8388608
  622.3 9.5 %copy-start.1 = (bf16[40,1024]{1,0:T(8,128)(2,1)S(1)}, bf16[40,1024]{1,0:T(8,128)(2,1)}, u32[]{:S(2)}) copy-start(bf16[40,1024]{1,0:T(8,128)(2,1)} %param.17) | copy-start | bytes 245764
  (6 other events, 23.4 us)
Sparse Core Ops, SparseCore 0:
  76.3 218.2 all-reduce.2
  296.8 80.6 all-gather.4
  475.1 140.2 all-gather.6
where the time goes:
time: 650 us; the launch traced here: 638 us
  waiting for transfers between devices  328 us (50%)
  blocking collectives  124 us (19%)
  local copies, waits for them, and re-layouts  77.2 us (12%)
  starting transfers between devices  38.9 us (6%)
  matrix products  28.7 us (4%)
  other arithmetic  27 us (4%)
  between operations  15 us (2%)
    all_gather x1, waiting for transfers between devices, shards(): lax.all_gather(local_heads, 'tensor', axis=2, tiled=True)  140 us
    unnamed x4, waiting for transfers between devices  118 us
    all_gather x1, blocking collectives, shards(): lax.all_gather(norm_gain, 'tensor', axis=0, tiled=True)  97.5 us
    all_to_all x1, waiting for transfers between devices, shards(): lax.all_to_all(spread(w_key, replicas, owners), ('dp', 'tensor'), split_a...  35.2 us
    all_to_all x1, waiting for transfers between devices, shards(): lax.all_to_all(spread(w_value, replicas, owners), ('dp', 'tensor'), split...  34.2 us
    gather x2, local copies, waits for them, and re-layouts, shards(): jnp.take(embed_table, jnp.clip(local_id, 0, vocab_rows - 1), axis=0)  31.1 us
    all_gather x1, blocking collectives, shards(): every_id = lax.all_gather(token_ids, 'dp', axis=0, tiled=True)  26.1 us
    all_to_all x1, starting transfers between devices, shards(): lax.all_to_all(spread(w_out, replicas, owners), ('dp', 'tensor'), split_a...  17.3 us
  transfers between devices with their start and end apart: 7, of which 4 were waited for; matrix products, arithmetic and copies ran while one was open for 12% of the time, Pallas kernels for 0%

commit v1 on v0

v1 whole, which is shorter than its diff:
```python
import math

import jax
import jax.numpy as jnp
from jax import lax
from jax.experimental import pallas as pl
from jax.experimental.pallas import tpu as pltpu
from jax.sharding import PartitionSpec as P

EPS = 1e-06
THETA = 1000000.0
SLOTS = 64
LANES = 128
EXTRA = 16
MESH = pl.DeviceIdType.MESH
NT = (((1,), (1,)), ((), ()))


class Place:
    def __init__(self):
        self.dp = lax.axis_index("dp")
        self.t = lax.axis_index("tensor")
        self.y, self.xh, self.c = self.dp // 4, (self.dp // 2) % 2, self.dp % 2
        self.xl, self.z = self.t // 4, self.t % 4

    def dp_id(self, dy, dxh, dc=0):
        return ((self.y + dy) % 4) * 4 + ((self.xh + dxh) % 2) * 2 + (self.c + dc) % 2

    def t_id(self, dxl, dz):
        return ((self.xl + dxl) % 2) * 4 + (self.z + dz) % 4


def remote(src, dst, sems, k, device):
    return pltpu.make_async_remote_copy(
        src_ref=src,
        dst_ref=dst,
        send_sem=sems.at[0, k],
        recv_sem=sems.at[1, k],
        device_id=device,
        device_id_type=MESH,
    )


def greet(devices):
    barrier = pltpu.get_barrier_semaphore()
    for device in devices:
        pl.semaphore_signal(barrier, inc=1, device_id=device, device_id_type=MESH)
    pl.semaphore_wait(barrier, len(devices))


class PairRing:
    COPIES = 9

    def __init__(self, own, block, first, second, ident, device, sems, landed=None):
        self.landed = landed or (lambda k, e: None)
        self.ident = ident
        pair, nxt, prv = device(0, 1), device(1, 0), device(3, 0)
        me, mate = ident(0, 0), ident(0, 1)
        self.c = [
            remote(own, block(me), sems, 0, pair),
            remote(own, block(me), sems, 1, nxt),
            remote(own, block(me), sems, 2, prv),
            remote(block(mate), block(mate), sems, 3, nxt),
            remote(block(mate), block(mate), sems, 4, prv),
            remote(first(ident(3, 0)), first(ident(3, 0)), sems, 5, nxt),
            remote(second(ident(1, 0)), second(ident(1, 0)), sems, 6, prv),
            remote(first(ident(3, 1)), first(ident(3, 1)), sems, 7, nxt),
            remote(second(ident(1, 1)), second(ident(1, 1)), sems, 8, prv),
        ]

    def s0(self):
        self.c[0].start()
        self.c[1].start()
        self.c[2].start()

    def s1(self):
        self.c[0].wait_recv()
        self.c[3].start()
        self.c[4].start()
        self.landed(0, 1)

    def s2(self):
        self.c[1].wait_recv()
        self.c[5].start()
        self.landed(3, 0)
        self.c[2].wait_recv()
        self.c[6].start()
        self.landed(1, 0)

    def s3(self):
        self.c[3].wait_recv()
        self.c[7].start()
        self.landed(3, 1)
        self.c[4].wait_recv()
        self.c[8].start()
        self.landed(1, 1)

    def s4(self):
        self.c[5].wait_recv()
        self.c[6].wait_recv()
        self.landed(2, 0)
        self.c[7].wait_recv()
        self.c[8].wait_recv()
        self.landed(2, 1)

    def end(self):
        for copy in self.c:
            copy.wait_send()


class CoreShare:
    COPIES = 8

    def __init__(self, block, place, sems):
        self.block, self.place, self.sems = block, place, sems
        self.started = []

    def give(self, src, k, e):
        p = self.place
        copy = remote(
            src, self.block(p.dp_id(k, e)), self.sems, k * 2 + e, (p.dp_id(0, 0, 1), p.t)
        )
        copy.start()
        self.started.append(copy)

    def end(self):
        for copy in self.started:
            copy.wait()


def fetch_kernel(
    req, slot, gain, table, wq, wk, wv, wo,
    w_all, wo_part, e_all, flag,
    reqs, table_v, index_v, slots_out, slots_in, e_own,
    req_sems, slot_sems, p1_sems, o1_sems, ring_sems, core_sems, e_sems, local_sems,
):
    p = Place()
    dp, t = p.dp, p.t
    owners, tensors = reqs.shape[0], e_all.shape[0]
    vocab = table.shape[0]
    qw, kw = wq.shape[1] // tensors, wk.shape[1] // tensors
    ow = wo.shape[1] // tensors
    dp_peers = [(lax.rem(dp + j, owners), t) for j in range(1, owners)]
    t_peers = [(dp, lax.rem(t + j, tensors)) for j in range(1, tensors)]
    greet(dp_peers + t_peers)

    asks = []
    for j in range(1, owners):
        to = lax.rem(dp + j, owners)
        copy = remote(req.at[to], reqs.at[dp], req_sems, j, (to, t))
        copy.start()
        asks.append(copy)
    own_ask = pltpu.make_async_copy(req.at[dp], reqs.at[dp], local_sems.at[0])
    own_ask.start()
    load_table = pltpu.make_async_copy(table, table_v.at[pl.ds(0, vocab)], local_sems.at[1])
    load_table.start()

    row = dp * tensors + t
    parts = ((wq, qw, 0), (wk, kw, qw), (wv, kw, qw + kw))
    first = []
    for j in range(1, tensors):
        to = lax.rem(t + j, tensors)
        for a, (w, n, at) in enumerate(parts):
            copy = remote(
                w.at[:, pl.ds(pl.multiple_of(to * n, LANES), n)],
                w_all.at[row, :, pl.ds(at, n)],
                p1_sems, j * 3 + a, (dp, to),
            )
            copy.start()
            first.append(copy)
    stays = []
    for a, (w, n, at) in enumerate(parts):
        copy = pltpu.make_async_copy(
            w.at[:, pl.ds(pl.multiple_of(t * n, LANES), n)],
            w_all.at[row, :, pl.ds(at, n)],
            local_sems.at[2 + a],
        )
        copy.start()
        stays.append(copy)
    copy = pltpu.make_async_copy(
        wo.at[:, pl.ds(pl.multiple_of(t * ow, LANES), ow)], wo_part.at[t], local_sems.at[5]
    )
    copy.start()
    stays.append(copy)

    pad = table_v.shape[0] - vocab
    table_v[pl.ds(vocab, pad), :] = jnp.zeros((pad, table_v.shape[1]), table_v.dtype)
    for copy in asks:
        copy.wait_recv()
    own_ask.wait()
    asked = jnp.concatenate(
        [reqs[lax.rem(dp + j, owners), 0:1, :] for j in range(owners)], axis=0
    )
    over = jnp.max(jnp.where(lax.broadcasted_iota(jnp.int32, asked.shape, 1) == SLOTS, asked, 0))
    flag[...] = jnp.full(flag.shape, over, jnp.int32)
    columns = jnp.transpose(asked)
    for j in range(owners):
        index_v[j * SLOTS:(j + 1) * SLOTS, :] = jnp.broadcast_to(
            columns[:SLOTS, j:j + 1], (SLOTS, LANES)
        )
    load_table.wait()
    chunk = 4
    replies = []
    for m in range(owners // chunk):
        wanted = index_v[m * chunk * SLOTS:(m + 1) * chunk * SLOTS, 0:1]
        place = lax.broadcasted_iota(jnp.int32, (chunk * SLOTS, table_v.shape[0]), 1)
        hit = (place == wanted).astype(jnp.float32).astype(jnp.bfloat16)
        rows = jnp.dot(hit, table_v[...], preferred_element_type=jnp.float32)
        slots_out[m * chunk:(m + 1) * chunk] = rows.astype(jnp.bfloat16).reshape(
            chunk, SLOTS, rows.shape[1]
        )
        for j in range(m * chunk, (m + 1) * chunk):
            if j == 0:
                copy = pltpu.make_async_copy(slots_out.at[0], slots_in.at[dp], local_sems.at[6])
            else:
                copy = remote(
                    slots_out.at[j], slots_in.at[dp], slot_sems, j, (lax.rem(dp + j, owners), t)
                )
            copy.start()
            replies.append(copy)

    for copy in first:
        copy.wait_recv()
    for copy in stays:
        copy.wait()

    def block(i):
        return w_all.at[pl.ds(i * tensors, tensors)]

    half = tensors // 2
    share = CoreShare(block, p, core_sems)
    ring = PairRing(
        block(dp),
        block,
        lambda i: w_all.at[pl.ds(i * tensors, half)],
        lambda i: w_all.at[pl.ds(i * tensors + half, half)],
        lambda k, e: p.dp_id(k, e),
        lambda k, e: (p.dp_id(k, e), t),
        ring_sems,
        lambda k, e: share.give(block(p.dp_id(k, e)), k, e),
    )
    ring.s0()
    share.give(block(dp), 0, 0)

    replies[0].wait()
    for copy in replies[1:]:
        copy.wait_recv()
    picks = lax.broadcasted_iota(jnp.int32, (slot.shape[0], owners * SLOTS), 1) == slot[...]
    tokens = slot.shape[0]
    e_own[0:tokens] = jnp.dot(
        picks.astype(jnp.float32).astype(jnp.bfloat16),
        slots_in[...].reshape(owners * SLOTS, slots_in.shape[2]),
        preferred_element_type=jnp.float32,
    ).astype(jnp.bfloat16)
    e_own[tokens:] = jnp.broadcast_to(gain[...], (EXTRA, gain.shape[1]))
    e_ring = PairRing(
        e_own,
        lambda i: e_all.at[i],
        lambda i: e_all.at[i, pl.ds(0, tokens // 2)],
        lambda i: e_all.at[i, pl.ds(tokens // 2, tokens // 2 + EXTRA)],
        lambda k, e: p.t_id(e, k),
        lambda k, e: (dp, p.t_id(e, k)),
        e_sems,
    )
    e_ring.s0()
    keep = pltpu.make_async_copy(e_own, e_all.at[t], local_sems.at[7])
    keep.start()
    ring.s1()
    e_ring.s1()
    e_ring.s2()
    ring.s2()
    e_ring.s3()
    outs = []
    for j in range(1, tensors):
        to = lax.rem(t + j, tensors)
        copy = remote(
            wo.at[:, pl.ds(pl.multiple_of(to * ow, LANES), ow)],
            wo_part.at[t],
            o1_sems, j, (dp, to),
        )
        copy.start()
        outs.append(copy)
    ring.s3()
    e_ring.s4()
    ring.s4()
    for copy in outs:
        copy.wait()
    for copy in first + asks + replies[1:]:
        copy.wait_send()
    keep.wait()
    ring.end()
    e_ring.end()
    share.end()


def fetch(req, slot, gain, table, wq, wk, wv, wo):
    owners, tensors = lax.axis_size("dp"), lax.axis_size("tensor")
    tokens = slot.shape[0]
    features = table.shape[1]
    height, depth = wq.shape[0], wo.shape[0]
    wide = (wq.shape[1] + wk.shape[1] + wv.shape[1]) // tensors
    padded = -(-table.shape[0] // LANES) * LANES
    anywhere, vmem = pl.BlockSpec(memory_space=pl.ANY), pl.BlockSpec(memory_space=pltpu.VMEM)
    dma = pltpu.SemaphoreType.DMA
    bf16 = jnp.bfloat16
    return pl.pallas_call(
        fetch_kernel,
        out_shape=(
            jax.ShapeDtypeStruct((owners * tensors, height, wide), bf16),
            jax.ShapeDtypeStruct((tensors, depth, wo.shape[1] // tensors), bf16),
            jax.ShapeDtypeStruct((tensors, tokens + EXTRA, features), bf16),
            jax.ShapeDtypeStruct((8, LANES), jnp.int32),
        ),
        in_specs=[anywhere, vmem, vmem] + [anywhere] * 5,
        out_specs=(anywhere, anywhere, anywhere, vmem),
        scratch_shapes=[
            pltpu.VMEM((owners, 8, LANES), jnp.int32),
            pltpu.VMEM((padded, features), bf16),
            pltpu.VMEM((owners * SLOTS, LANES), jnp.int32),
            pltpu.VMEM((owners, SLOTS, features), bf16),
            pltpu.VMEM((owners, SLOTS, features), bf16),
            pltpu.VMEM((tokens + EXTRA, features), bf16),
            dma((2, owners)),
            dma((2, owners)),
            dma((2, 3 * tensors)),
            dma((2, tensors)),
            dma((2, PairRing.COPIES)),
            dma((2, CoreShare.COPIES)),
            dma((2, PairRing.COPIES)),
            dma((8,)),
        ],
        compiler_params=pltpu.CompilerParams(
            collective_id=1, has_side_effects=True, vmem_limit_bytes=40 * 1024 * 1024
        ),
        name="fetch",
    )(req, slot, gain, table, wq, wk, wv, wo)


ROWS_AT_ONCE = 4
PIECES = 4


def block_kernel(
    lengths, e_all, w_all, wo_part, q_gain, k_gain, cosine, sine, key_cache, value_cache,
    attended, new_keys, new_values,
    e_v, w_v, wo_v, heads_v, acc_v, nk_v, nv_v, k_v, v_v, total_v,
    w_sems, kv_sems, ring_sems, core_sems, heads_sems, local_sems,
):
    p = Place()
    dp, t = p.dp, p.t
    tensors, features = e_v.shape[0], e_v.shape[2]
    tokens = attended.shape[0]
    width = LANES
    rows, cache = key_cache.shape[0], key_cache.shape[1]
    steps = tokens // rows
    qw = heads_v.shape[2]
    heads = qw // width
    greet(
        [(p.dp_id(0, 0, 1), t), (p.dp_id(0, 1), t), (p.dp_id(1, 0), t), (p.dp_id(3, 0), t)]
        + [(dp, p.t_id(1, 0)), (dp, p.t_id(0, 1)), (dp, p.t_id(0, 3))]
    )

    load_e = pltpu.make_async_copy(e_all, e_v, local_sems.at[0])
    load_e.start()
    loads = [pltpu.make_async_copy(w_all.at[i], w_v.at[i], w_sems.at[i]) for i in range(tensors)]
    for copy in loads:
        copy.start()

    def block(i):
        return wo_v.at[pl.ds(i * tensors, tensors)]

    half = tensors // 2
    share = CoreShare(block, p, core_sems)
    ring = PairRing(
        wo_part,
        block,
        lambda i: wo_v.at[pl.ds(i * tensors, half)],
        lambda i: wo_v.at[pl.ds(i * tensors + half, half)],
        lambda k, e: p.dp_id(k, e),
        lambda k, e: (p.dp_id(k, e), t),
        ring_sems,
        lambda k, e: share.give(block(p.dp_id(k, e)), k, e),
    )
    ring.s0()
    share.give(wo_part, 0, 0)
    keep = pltpu.make_async_copy(wo_part, block(dp), local_sems.at[1])
    keep.start()

    piece = rows // PIECES

    def load_kv(i):
        at = pl.ds(i * piece, piece)
        return (
            pltpu.make_async_copy(key_cache.at[at], k_v.at[i % 2], kv_sems.at[0, i]),
            pltpu.make_async_copy(value_cache.at[at], v_v.at[i % 2], kv_sems.at[1, i]),
        )

    caches = [load_kv(i) for i in range(PIECES)]
    for copy in caches[0] + caches[1]:
        copy.start()

    load_e.wait()

    def square(i, total):
        wide = e_v[i, pl.ds(0, tokens)].astype(jnp.float32)
        return total + jnp.sum(wide * wide, axis=-1, keepdims=True)

    total = lax.fori_loop(0, tensors, square, jnp.zeros((tokens, 1), jnp.float32))
    inverse = lax.rsqrt(total / (tensors * features) + EPS)
    for i in range(tensors):
        loads[i].wait()

    def project(i, carry):
        gain = e_v[i, pl.ds(tokens, EXTRA)].astype(jnp.float32)[0:1]
        normed = e_v[i, pl.ds(0, tokens)].astype(jnp.float32) * inverse * gain
        part = jnp.dot(normed.astype(jnp.bfloat16), w_v[i], preferred_element_type=jnp.float32)
        acc_v[...] = acc_v[...] + part
        return carry

    acc_v[...] = jnp.zeros(acc_v.shape, jnp.float32)
    lax.fori_loop(0, tensors, project, 0)

    def placed(raw, head_gain):
        mean_sq = jnp.mean(raw * raw, axis=-1, keepdims=True)
        scaled = raw * lax.rsqrt(mean_sq + EPS) * head_gain
        return scaled * cosine[...] + pltpu.roll(scaled, width // 2, 1) * sine[...]

    head_gain = q_gain[...].astype(jnp.float32)
    for h in range(heads):
        at = slice(h * width, (h + 1) * width)
        acc_v[:, at] = placed(acc_v[:, at], head_gain)
    nk_v[...] = placed(acc_v[:, qw:qw + width], k_gain[...].astype(jnp.float32)).astype(jnp.bfloat16)
    nv_v[...] = acc_v[:, qw + width:qw + 2 * width].astype(jnp.bfloat16)
    new_keys[...] = nk_v[...]
    new_values[...] = nv_v[...]
    ring.s1()

    scale = 1.0 / math.sqrt(width)
    pair = 2 * steps
    group = ROWS_AT_ONCE * steps
    query = lax.broadcasted_iota(jnp.int32, (heads * pair, 1), 0) % pair
    is_first = query < steps
    fresh = lax.broadcasted_iota(jnp.int32, (heads * pair, group), 1)
    column = lax.broadcasted_iota(jnp.int32, (heads * pair, cache), 1)

    def attend(i, g):
        at = pl.ds(pl.multiple_of(i * piece * steps + g * group, group), group)
        queries = acc_v[at, 0:qw]
        keys, values = nk_v[at, :], nv_v[at, :]
        results = []
        for n in range(ROWS_AT_ONCE // 2):
            q = jnp.concatenate(
                [
                    queries[n * pair:(n + 1) * pair, h * width:(h + 1) * width]
                    for h in range(heads)
                ],
                axis=0,
            ).astype(jnp.bfloat16)
            r = g * ROWS_AT_ONCE + 2 * n
            old_a = lax.dot_general(q, k_v[i % 2, r], NT, preferred_element_type=jnp.float32)
            old_b = lax.dot_general(q, k_v[i % 2, r + 1], NT, preferred_element_type=jnp.float32)
            new = lax.dot_general(q, keys, NT, preferred_element_type=jnp.float32) * scale
            token = query + n * pair
            new = jnp.where((fresh // steps == token // steps) & (fresh <= token), new, -jnp.inf)
            held = jnp.where(
                is_first, lengths[i * piece + r], lengths[i * piece + r + 1]
            )
            old = jnp.where(is_first, old_a, old_b) * scale
            old = jnp.where(column < held, old, -jnp.inf)
            top = jnp.maximum(
                jnp.max(old, axis=-1, keepdims=True), jnp.max(new, axis=-1, keepdims=True)
            )
            old = jnp.exp(old - top)
            new = jnp.exp(new - top)
            whole = jnp.sum(old, axis=-1, keepdims=True) + jnp.sum(new, axis=-1, keepdims=True)
            inv = 1.0 / whole
            old = (old * inv).astype(jnp.bfloat16)
            new = (new * inv).astype(jnp.bfloat16)
            out_a = jnp.dot(old, v_v[i % 2, r], preferred_element_type=jnp.float32)
            out_b = jnp.dot(old, v_v[i % 2, r + 1], preferred_element_type=jnp.float32)
            out = jnp.where(is_first, out_a, out_b)
            out = out + jnp.dot(new, values, preferred_element_type=jnp.float32)
            results.append(
                jnp.concatenate([out[h * pair:(h + 1) * pair] for h in range(heads)], axis=1)
            )
        heads_v[t, at, :] = jnp.concatenate(results, axis=0).astype(jnp.bfloat16)

    halves = 2
    span = tokens // halves
    rings = []
    for j in range(halves):
        rings.append(
            PairRing(
                heads_v.at[t, pl.ds(j * span, span)],
                lambda i, j=j: heads_v.at[i, pl.ds(j * span, span)],
                lambda i, j=j: heads_v.at[i, pl.ds(j * span, span // 2)],
                lambda i, j=j: heads_v.at[i, pl.ds(j * span + span // 2, span // 2)],
                lambda k, e: p.t_id(e, k),
                lambda k, e: (dp, p.t_id(e, k)),
                heads_sems.at[j],
            )
        )
    for i in range(PIECES):
        for copy in caches[i]:
            copy.wait()

        def one(g, carry):
            attend(i, g)
            return carry

        lax.fori_loop(0, piece // ROWS_AT_ONCE, one, 0)
        if i + 2 < PIECES:
            for copy in caches[i + 2]:
                copy.start()
        if i == PIECES // 2 - 1:
            rings[0].s0()
            ring.s2()
        if i == PIECES // 2:
            rings[0].s1()
    rings[1].s0()
    rings[0].s2()
    ring.s3()
    rings[1].s1()
    rings[0].s3()
    rings[1].s2()
    rings[1].s3()
    ring.s4()
    rings[0].s4()
    rings[1].s4()
    keep.wait()
    share.end()

    def back(i, carry):
        w = wo_v[pl.ds(i * (owners_per(tensors, wo_v)), owners_per(tensors, wo_v))]
        w = w.reshape(qw, w.shape[-1])
        total_v[...] = total_v[...] + jnp.dot(heads_v[i], w, preferred_element_type=jnp.float32)
        return carry

    total_v[...] = e_v[t, pl.ds(0, tokens)].astype(jnp.float32)
    lax.fori_loop(0, tensors, back, 0)
    attended[...] = total_v[...].astype(jnp.bfloat16)
    ring.end()
    rings[0].end()
    rings[1].end()


def owners_per(tensors, wo_v):
    return wo_v.shape[0] // tensors


def decode(lengths, e_all, w_all, wo_part, q_gain, k_gain, cosine, sine, keys, values):
    owners, tensors = lax.axis_size("dp"), lax.axis_size("tensor")
    held, features = e_all.shape[1:]
    tokens = held - EXTRA
    rows, cache, width = keys.shape
    wide = w_all.shape[-1]
    depth, ow = wo_part.shape[1:]
    qw = wide - 2 * width
    piece = rows // PIECES
    anywhere, vmem = pl.BlockSpec(memory_space=pl.ANY), pl.BlockSpec(memory_space=pltpu.VMEM)
    smem = pl.BlockSpec(memory_space=pltpu.SMEM)
    dma = pltpu.SemaphoreType.DMA
    bf16, f32 = jnp.bfloat16, jnp.float32
    return pl.pallas_call(
        block_kernel,
        out_shape=(
            jax.ShapeDtypeStruct((tokens, ow), bf16),
            jax.ShapeDtypeStruct((tokens, width), bf16),
            jax.ShapeDtypeStruct((tokens, width), bf16),
        ),
        in_specs=[smem, anywhere, anywhere, anywhere] + [vmem] * 4 + [anywhere] * 2,
        out_specs=(vmem, vmem, vmem),
        scratch_shapes=[
            pltpu.VMEM((tensors, held, features), bf16),
            pltpu.VMEM((tensors, features, wide), bf16),
            pltpu.VMEM((owners * tensors, depth, ow), bf16),
            pltpu.VMEM((tensors, tokens, qw), bf16),
            pltpu.VMEM((tokens, wide), f32),
            pltpu.VMEM((tokens, width), bf16),
            pltpu.VMEM((tokens, width), bf16),
            pltpu.VMEM((2, piece, cache, width), bf16),
            pltpu.VMEM((2, piece, cache, width), bf16),
            pltpu.VMEM((tokens, ow), f32),
            dma((tensors,)),
            dma((2, PIECES)),
            dma((2, PairRing.COPIES)),
            dma((2, CoreShare.COPIES)),
            dma((2, 2, PairRing.COPIES)),
            dma((2,)),
        ],
        compiler_params=pltpu.CompilerParams(
            collective_id=2, has_side_effects=True, vmem_limit_bytes=56 * 1024 * 1024
        ),
        name="decode",
    )(lengths, e_all, w_all, wo_part, q_gain, k_gain, cosine, sine, keys, values)


def requests(ids, vocab_rows, owners):
    count = ids.shape[0]
    owner = ids // vocab_rows
    before = jnp.arange(count)[None, :] < jnp.arange(count)[:, None]
    rank = jnp.sum((owner[:, None] == owner[None, :]) & before, axis=1, dtype=jnp.int32)
    over = jnp.any(rank >= SLOTS).astype(jnp.int32)
    mine = (owner[None, None, :] == jnp.arange(owners)[:, None, None]) & (
        rank[None, None, :] == jnp.arange(SLOTS)[None, :, None]
    )
    wanted = jnp.max(jnp.where(mine, (ids - owner * vocab_rows)[None, None, :], -1), axis=-1)
    rest = jnp.full((owners, LANES - SLOTS), over, jnp.int32)
    asked = jnp.concatenate([wanted, rest], axis=1)
    req = jnp.broadcast_to(asked[:, None, :], (owners, 8, LANES))
    return req, (owner * SLOTS + rank)[:, None]


def all_embeddings(token_ids, embed_table, extra):
    rows, steps = token_ids.shape
    every_id = lax.all_gather(token_ids, "dp", axis=0, tiled=True)
    vocab_rows = embed_table.shape[0]
    local_id = every_id - lax.axis_index("dp") * vocab_rows
    inside = (local_id >= 0) & (local_id < vocab_rows)
    picked = jnp.take(embed_table, jnp.clip(local_id, 0, vocab_rows - 1), axis=0)
    partial_rows = jnp.where(inside[..., None], picked, jnp.zeros((), jnp.bfloat16))
    own = lax.psum_scatter(partial_rows, "dp", scatter_dimension=0, tiled=True)
    own = own.reshape(rows * steps, -1)
    return jnp.concatenate([lax.all_gather(own, "tensor", axis=0, tiled=False), extra], axis=1)


def shards(
    token_ids,
    lengths,
    embed_table,
    norm_gain,
    w_query,
    w_key,
    w_value,
    w_out,
    q_gain,
    k_gain,
    key_cache,
    value_cache,
):
    owners, tensors = lax.axis_size("dp"), lax.axis_size("tensor")
    rows, steps = token_ids.shape
    width = q_gain.shape[0]
    features = embed_table.shape[1]
    req, slot = requests(token_ids.reshape(-1), embed_table.shape[0], owners)
    positions = (lengths[:, None] + jnp.arange(steps, dtype=jnp.int32)[None, :]).reshape(-1)
    half = width // 2
    freq = THETA ** (-jnp.arange(half, dtype=jnp.float32) * 2.0 / width)
    angle = positions.astype(jnp.float32)[:, None] * freq
    cosine, sine = jnp.cos(angle), jnp.sin(angle)
    cosine = jnp.concatenate([cosine, cosine], axis=-1)
    sine = jnp.concatenate([-sine, sine], axis=-1)
    w_all, wo_part, e_all, flag = fetch(
        req, slot, norm_gain[None], embed_table, w_query, w_key, w_value, w_out
    )
    e_all = lax.cond(
        flag[0, 0] > 0,
        lambda kept: all_embeddings(token_ids, embed_table, kept[:, rows * steps:]),
        lambda kept: kept,
        e_all,
    )
    w_all = w_all.reshape(tensors, features, w_all.shape[-1])
    attended, new_keys, new_values = decode(
        lengths, e_all, w_all, wo_part, q_gain[None], k_gain[None],
        cosine, sine, key_cache, value_cache,
    )
    return (
        attended.reshape(rows, steps, -1),
        new_keys.reshape(rows, steps, -1),
        new_values.reshape(rows, steps, -1),
    )


def solution(mesh):
    in_specs = (
        P("dp", None),
        P("dp"),
        P("dp", "tensor"),
        P("tensor"),
        P(("dp", "tensor"), None),
        P(("dp", "tensor"), None),
        P(("dp", "tensor"), None),
        P(("dp", "tensor"), None),
        P(),
        P(),
        P("dp", None, "tensor"),
        P("dp", None, "tensor"),
    )
    out_specs = (P("dp", None, "tensor"), P("dp", None, "tensor"), P("dp", None, "tensor"))
    return jax.shard_map(shards, mesh=mesh, in_specs=in_specs, out_specs=out_specs, check_vma=False)
```

time: 650 us -> 199 us (0.31); the launches traced: 638 us -> 198 us
  waiting for transfers between devices: 328 us -> 0 us
  Pallas kernels: 0 us -> 165 us
  blocking collectives: 124 us -> 0 us
  local copies, waits for them, and re-layouts: 77.2 us -> 12.7 us
  starting transfers between devices: 38.9 us -> 0 us
  matrix products: 28.7 us -> 0 us
  other arithmetic: 27 us -> 4.09 us
    pallas_call x0 -> x2, Pallas kernels: none -> 165 us  [the longest x1 92.9 us: fetch(): pl.pallas_call(fetch_kernel, out_shape=(jax.ShapeDtypeStruct((owners * te...]
    all_gather x2 -> x0, waiting for transfers between devices: 140 us -> none  [the longest x1 140 us: shards(): lax.all_gather(local_heads, 'tensor', axis=2, tiled=True)]
    all_gather x2 -> x0, blocking collectives: 124 us -> none  [the longest x1 97.5 us: shards(): lax.all_gather(norm_gain, 'tensor', axis=0, tiled=True)]
    unnamed x4 -> x0, waiting for transfers between devices: 118 us -> none
    all_to_all x4 -> x0, waiting for transfers between devices: 69.4 us -> none  [the longest x1 35.2 us: shards(): lax.all_to_all(spread(w_key, replicas, owners), ('dp', 'tensor'), split_a...]
    all_to_all x4 -> x0, starting transfers between devices: 38.5 us -> none  [the longest x1 17.3 us: shards(): lax.all_to_all(spread(w_out, replicas, owners), ('dp', 'tensor'), split_a...]
    gather x2 -> x0, local copies, waits for them, and re-layouts: 31.1 us -> none  [shards(): jnp.take(embed_table, jnp.clip(local_id, 0, vocab_rows - 1), axis=0)]
    dot_general x8 -> x0, matrix products: 28.7 us -> none  [the longest x1 8.71 us: shards(): jnp.dot(all_heads, out_local, preferred_element_type=jnp.float32)]
  transfers between devices with their start and end apart: 7 -> 0, of which waited for: 4 -> 0; matrix products, arithmetic and copies ran while one was open for 12% -> 0% of each run, Pallas kernels for 0% -> 0%
where the time goes in v1:
time: 199 us; the launch traced here: 198 us
  Pallas kernels  165 us (83%)
  between operations  15.5 us (8%)
  local copies, waits for them, and re-layouts  12.7 us (6%)
  other arithmetic  4.09 us (2%)
    pallas_call x1, Pallas kernels, fetch(): pl.pallas_call(fetch_kernel, out_shape=(jax.ShapeDtypeStruct((owners * te...  92.9 us
    pallas_call x1, Pallas kernels, decode(): pl.pallas_call(block_kernel, out_shape=(jax.ShapeDtypeStruct((tokens, ow)...  72.3 us
    unnamed x17, local copies, waits for them, and re-layouts  9.01 us

profile of v1, /device:TPU:1, one launch (start us, length us, event | category | flops | bytes accessed | tf_op | source)
XLA Modules:
  0.0 197.8 jit_solution(15561086648310733773)
XLA Ops:
  7.2 0.8 copy.61
  8.1 0.2 convert_reduce_fusion
  8.4 0.3 select_reduce_fusion
  8.7 0.6 compare_reduce_fusion
  10.0 0.1 copy.68
  10.2 0.7 broadcast_divide_fusion
  11.1 0.7 fusion.5
  11.8 0.1 copy.62
  12.0 0.7 broadcast_in_dim.70.gain
  12.7 1.1 copy-done
  13.8 1.1 copy-done.1
  14.9 0.9 copy-done.3
  15.8 0.9 copy-done.4
  16.7 92.9 %fetch.1 = (bf16[128,40,1280]{2,1,0:T(8,128)(2,1)}, bf16[8,64,640]{2,1,0:T(8,128)(2,1)S(1)}, bf16[8,272,640]{2,1,0:T(8,128)(2,1)S(1)}, s32[8,128]{1,0:T(8,128)S(1)}) custom-call(s32[16,8,128]{2,1,0:T(8,128)S(1)} %broadcast_in_dim.69.req, s32[256,1]{1,0:T(8,128)S(1)} %fusion.3.slot, bf16[1,640]{1,0:T(2,128)(2,1)S(1)} %broadcast_in_dim.70.gain, ...), custom_call_target="tpu_custom_call" | custom-call | tf_op jit(solution)/shard_map/fetch/pallas_call | solution.py:306
  109.6 0.8 copy-done.2
  110.4 0.5 slice.6
  111.6 0.2 conditional.1
  111.9 0.4 copy-done.6
  112.5 0.5 fusion.4
  113.0 0.8 pad_maximum_fusion.1
  113.8 72.3 %decode.1 = (bf16[256,640]{1,0:T(8,128)(2,1)}, bf16[256,128]{1,0:T(8,128)(2,1)}, bf16[256,128]{1,0:T(8,128)(2,1)}) custom-call(s32[64]{0:T(128)} %lengths.1, bf16[8,272,640]{2,1,0:T(8,128)(2,1)S(1)} %get-tuple-element.49.e_all, bf16[8,640,1280]{2,1,0:T(8,128)(2,1)} %bitcast.12, bf16[8,64,640]{2,1,0:T(8,128)(2,1)} %copy-done.2, bf16[1,128]{1,0:T(2,128)(2,1)} %bitcast.18, ...), custom_call_target="tpu_custom_call" | custom-call | tf_op jit(solution)/shard_map/decode/pallas_call | solution.py:564
  186.2 1.8 reshape.224
  188.0 1.5 copy.80
  189.4 1.5 copy.81
  (21 shorter events, 0.7 us)
Async XLA Ops:
  7.2 104.4 %copy-start.5 = (s32[64,4]{0,1:T(4,128)S(1)}, s32[64,4]{0,1:T(4,128)}, u32[]{:S(2)}) copy-start(s32[64,4]{0,1:T(4,128)} %param.14) | copy-start | bytes 3076
  12.7 1.1 copy-start
  13.8 1.1 copy-start.1
  14.9 0.9 copy-start.3
  15.8 0.9 copy-start.4
  109.6 0.8 copy-start.2
  111.6 0.7 copy-start.6

commit v2 on v0

v2 whole, which is shorter than its diff:
```python
import math

import jax
import jax.numpy as jnp
import numpy as np
from jax import lax
from jax.experimental import pallas as pl
from jax.experimental.pallas import tpu as pltpu
from jax.sharding import PartitionSpec as P

EPS = 1e-06
THETA = 1000000.0
ROWS_AT_ONCE = 4
PIECES = 4
SLOTS = 32
LANES = 128
EXTRA = 16
MESH = pl.DeviceIdType.MESH
NT = (((1,), (1,)), ((), ()))


class Place:
    def __init__(self):
        self.dp = lax.axis_index("dp")
        self.t = lax.axis_index("tensor")
        self.y, self.xh, self.c = self.dp // 4, (self.dp // 2) % 2, self.dp % 2
        self.xl, self.z = self.t // 4, self.t % 4

    def dp_id(self, dy, dxh, dc=0):
        return ((self.y + dy) % 4) * 4 + ((self.xh + dxh) % 2) * 2 + (self.c + dc) % 2

    def t_id(self, dxl, dz):
        return ((self.xl + dxl) % 2) * 4 + (self.z + dz) % 4


def remote(src, dst, sems, k, device):
    return pltpu.make_async_remote_copy(
        src_ref=src,
        dst_ref=dst,
        send_sem=sems.at[0, k],
        recv_sem=sems.at[1, k],
        device_id=device,
        device_id_type=MESH,
    )


def greet(devices):
    barrier = pltpu.get_barrier_semaphore()
    for device in devices:
        pl.semaphore_signal(barrier, inc=1, device_id=device, device_id_type=MESH)
    pl.semaphore_wait(barrier, len(devices))


class PairRing:
    COPIES = 9

    def __init__(self, own, block, first, second, ident, device, sems, landed=None):
        self.landed = landed or (lambda k, e: None)
        self.ident = ident
        pair, nxt, prv = device(0, 1), device(1, 0), device(3, 0)
        me, mate = ident(0, 0), ident(0, 1)
        self.c = [
            remote(own, block(me), sems, 0, pair),
            remote(own, block(me), sems, 1, nxt),
            remote(own, block(me), sems, 2, prv),
            remote(block(mate), block(mate), sems, 3, nxt),
            remote(block(mate), block(mate), sems, 4, prv),
            remote(first(ident(3, 0)), first(ident(3, 0)), sems, 5, nxt),
            remote(second(ident(1, 0)), second(ident(1, 0)), sems, 6, prv),
            remote(first(ident(3, 1)), first(ident(3, 1)), sems, 7, nxt),
            remote(second(ident(1, 1)), second(ident(1, 1)), sems, 8, prv),
        ]

    def s0(self):
        self.c[0].start()
        self.c[1].start()
        self.c[2].start()

    def s1(self):
        self.c[0].wait_recv()
        self.c[3].start()
        self.c[4].start()
        self.landed(0, 1)

    def s2(self):
        self.c[1].wait_recv()
        self.c[5].start()
        self.landed(3, 0)
        self.c[2].wait_recv()
        self.c[6].start()
        self.landed(1, 0)

    def s3(self):
        self.c[3].wait_recv()
        self.c[7].start()
        self.landed(3, 1)
        self.c[4].wait_recv()
        self.c[8].start()
        self.landed(1, 1)

    def s4(self):
        self.c[5].wait_recv()
        self.c[6].wait_recv()
        self.landed(2, 0)
        self.c[7].wait_recv()
        self.c[8].wait_recv()
        self.landed(2, 1)

    def end(self):
        for copy in self.c:
            copy.wait_send()


class RingPair:
    COPIES = 8

    def __init__(self, own, block, first, second, ident, device, sems, landed=None):
        self.landed = landed or (lambda k, e: None)
        pair, nxt, prv = device(0, 1), device(1, 0), device(3, 0)
        me = ident(0, 0)
        self.c = [
            remote(own, block(me), sems, 0, nxt),
            remote(own, block(me), sems, 1, prv),
            remote(first(ident(3, 0)), first(ident(3, 0)), sems, 2, nxt),
            remote(second(ident(1, 0)), second(ident(1, 0)), sems, 3, prv),
            remote(own, block(me), sems, 4, pair),
            remote(block(ident(3, 0)), block(ident(3, 0)), sems, 5, pair),
            remote(block(ident(1, 0)), block(ident(1, 0)), sems, 6, pair),
            remote(block(ident(2, 0)), block(ident(2, 0)), sems, 7, pair),
        ]

    def s0(self):
        self.c[0].start()
        self.c[1].start()
        self.c[4].start()

    def s1(self):
        self.c[0].wait_recv()
        self.c[2].start()
        self.c[5].start()
        self.landed(3, 0)
        self.c[1].wait_recv()
        self.c[3].start()
        self.c[6].start()
        self.landed(1, 0)

    def s2(self):
        self.c[2].wait_recv()
        self.c[3].wait_recv()
        self.c[7].start()
        self.landed(2, 0)

    def s3(self):
        self.c[4].wait_recv()
        self.landed(0, 1)
        self.c[5].wait_recv()
        self.landed(3, 1)
        self.c[6].wait_recv()
        self.landed(1, 1)

    def s4(self):
        self.c[7].wait_recv()
        self.landed(2, 1)

    def end(self):
        for copy in self.c:
            copy.wait_send()


class CoreShare:
    COPIES = 8

    def __init__(self, block, place, sems):
        self.block, self.place, self.sems = block, place, sems
        self.copies = {}

    def give(self, src, k, e):
        p = self.place
        copy = remote(
            src, self.block(p.dp_id(k, e)), self.sems, k * 2 + e, (p.dp_id(0, 0, 1), p.t)
        )
        copy.start()
        self.copies[k, e] = copy

    def took(self, k, e):
        self.copies[k, e].wait_recv()

    def end(self):
        for copy in self.copies.values():
            copy.wait_send()


class Columns:
    def __init__(self, own, blocks, count, place, ring_sems, share_sems):
        cut = count * 3 // 4
        rest = count - cut

        def made(kind, start, size, sems, share_sems):
            half = size // 2
            block = lambda i: blocks(i, start, size)
            share = CoreShare(block, place, share_sems)
            ring = kind(
                own(start, size),
                block,
                lambda i: blocks(i, start, half),
                lambda i: blocks(i, start + half, size - half),
                place.dp_id,
                lambda k, e: (place.dp_id(k, e), place.t),
                sems,
                lambda k, e: share.give(block(place.dp_id(k, e)), k, e),
            )
            return ring, share

        self.a, self.share_a = made(PairRing, 0, cut, ring_sems.at[0], share_sems.at[0])
        self.b, self.share_b = made(RingPair, cut, rest, ring_sems.at[1], share_sems.at[1])
        self.mine_a, self.mine_b = own(0, cut), own(cut, rest)

    def s0(self):
        self.a.s0()
        self.b.s0()
        self.share_a.give(self.mine_a, 0, 0)
        self.share_b.give(self.mine_b, 0, 0)

    def took(self, k, e):
        self.share_a.took(k, e)
        self.share_b.took(k, e)

    def end(self):
        self.a.end()
        self.b.end()
        self.share_a.end()
        self.share_b.end()


AROUND = ((0, 0), (0, 1), (1, 0), (3, 0), (1, 1), (3, 1), (2, 0), (2, 1))


def step_kernel(
    lengths, req, slot, gain, table, wq, wk, wv, wo, q_gain, k_gain, cosine, sine, key_cache, value_cache,
    attended, new_keys, new_values, flag, wa_all, wb_all,
    reqs, slot_v, gain_v, cos_v, sin_v, index_v, slots_out, slots_in, e_own, e_v, n_v, square_v,
    wa_v, wb_v, wo_part, wo_v, heads_v, acc_a, acc_b, nk_v, nv_v, k_v, v_v, total_v,
    req_sems, slot_sems, p1_sems, o1_sems, ring_sems, share_sems,
    e_sems, heads_sems, load_sems, kv_sems, local_sems,
):
    p = Place()
    dp, t = p.dp, p.t
    owners, tensors = reqs.shape[0], e_v.shape[0]
    tokens, features = attended.shape[0], e_v.shape[2]
    vocab = table.shape[0]
    height = wq.shape[0]
    width = LANES
    rows, cache = key_cache.shape[0], key_cache.shape[1]
    steps = tokens // rows
    qw, kw = wq.shape[1] // tensors, wk.shape[1] // tensors
    ow = wo.shape[1] // tensors
    heads = qw // width
    dp_peers = [(lax.rem(dp + j, owners), t) for j in range(1, owners)]
    t_peers = [(dp, lax.rem(t + j, tensors)) for j in range(1, tensors)]
    greet(dp_peers + t_peers)

    asks = []
    for j in range(1, owners):
        to = lax.rem(dp + j, owners)
        copy = remote(req.at[to], reqs.at[dp], req_sems, j, (to, t))
        copy.start()
        asks.append(copy)
    own_ask = pltpu.make_async_copy(req.at[dp], reqs.at[dp], local_sems.at[0])
    own_ask.start()

    stored = pl.ds(pl.multiple_of((dp * tensors + t) * height, 8), height)
    hw = qw // 2
    parts = (
        (wq, qw, 0, hw, wa_all, 0),
        (wk, kw, 0, kw, wa_all, hw),
        (wv, kw, 0, kw, wa_all, hw + kw),
        (wq, qw, hw, hw, wb_all, 0),
    )

    def columns_of(w, whole, at, n, to):
        return w.at[:, pl.ds(pl.multiple_of(to * whole + at, LANES), n)]

    first = ([], [])
    for half, some in enumerate((parts[:3], parts[3:])):
        for j in range(1, tensors):
            to = lax.rem(t + j, tensors)
            for a, (w, whole, at, n, into, column) in enumerate(some):
                copy = remote(
                    columns_of(w, whole, at, n, to),
                    into.at[stored, pl.ds(column, n)],
                    p1_sems, j * 4 + half * 3 + a, (dp, to),
                )
                copy.start()
                first[half].append(copy)
        if half == 0:
            load_table = pltpu.make_async_copy(
                table, wa_v.at[pl.ds(0, vocab), pl.ds(0, features)], local_sems.at[1]
            )
            load_table.start()
    stays = [
        pltpu.make_async_copy(
            columns_of(w, whole, at, n, t), into.at[stored, pl.ds(column, n)], local_sems.at[13 + a]
        )
        for a, (w, whole, at, n, into, column) in enumerate(parts)
    ]
    stays.append(
        pltpu.make_async_copy(
            wo.at[:, pl.ds(pl.multiple_of(t * ow, LANES), ow)], wo_part.at[t], local_sems.at[5]
        )
    )
    small = [
        pltpu.make_async_copy(a, b, local_sems.at[6 + i])
        for i, (a, b) in enumerate(((slot, slot_v), (gain, gain_v), (cosine, cos_v), (sine, sin_v)))
    ]
    for copy in stays + small:
        copy.start()

    padded = -(-vocab // LANES) * LANES
    wa_v[pl.ds(vocab, padded - vocab), pl.ds(0, features)] = jnp.zeros(
        (padded - vocab, features), wa_v.dtype
    )
    for copy in asks:
        copy.wait_recv()
    own_ask.wait()
    asked = jnp.concatenate(
        [reqs[lax.rem(dp + j, owners), 0:1, :] for j in range(owners)], axis=0
    )
    over = jnp.max(jnp.where(lax.broadcasted_iota(jnp.int32, asked.shape, 1) == SLOTS, asked, 0))
    flag[0, 0] = over
    columns = jnp.transpose(asked)
    for j in range(owners):
        index_v[j * SLOTS:(j + 1) * SLOTS, :] = jnp.broadcast_to(
            columns[:SLOTS, j:j + 1], (SLOTS, LANES)
        )
    load_table.wait()

    def columns(own, block, n):
        return Columns(own, block, tensors, p, ring_sems.at[n], share_sems.at[n])

    def in_projection(ref, n):
        def block(i, at, size):
            start = pl.multiple_of((i * tensors + at) * height, 8)
            return ref.at[pl.ds(start, size * height)]

        return columns(lambda at, size: block(dp, at, size), block, n)

    cols_a = in_projection(wa_all, 0)
    cols_b = in_projection(wb_all, 1)
    outs = columns(
        lambda at, size: wo_part.at[pl.ds(at, size)],
        lambda i, at, size: wo_v.at[pl.ds(i * tensors + at, size)],
        2,
    )

    chunk = 8
    replies = []
    for m in range(owners // chunk):
        wanted = index_v[m * chunk * SLOTS:(m + 1) * chunk * SLOTS, 0:1]
        place = lax.broadcasted_iota(jnp.int32, (chunk * SLOTS, padded), 1)
        hit = (place == wanted).astype(jnp.float32).astype(jnp.bfloat16)
        picked = jnp.dot(
            hit, wa_v[0:padded, 0:features], preferred_element_type=jnp.float32
        )
        slots_out[m * chunk:(m + 1) * chunk] = picked.astype(jnp.bfloat16).reshape(
            chunk, SLOTS, features
        )
        for j in range(m * chunk, (m + 1) * chunk):
            if j == 0:
                copy = pltpu.make_async_copy(slots_out.at[0], slots_in.at[dp], local_sems.at[10])
            else:
                copy = remote(
                    slots_out.at[j], slots_in.at[dp], slot_sems, j, (lax.rem(dp + j, owners), t)
                )
            copy.start()
            replies.append(copy)

    for copy in first[0]:
        copy.wait_recv()
    for copy in stays:
        copy.wait()
    cols_a.s0()
    second = []
    for j in range(1, tensors):
        to = lax.rem(t + j, tensors)
        copy = remote(
            wo.at[:, pl.ds(pl.multiple_of(to * ow, LANES), ow)],
            wo_part.at[t],
            o1_sems, j, (dp, to),
        )
        copy.start()
        second.append(copy)

    piece = rows // PIECES

    def load_kv(n):
        i = n % PIECES
        at = pl.ds(i * piece, piece)
        return (
            pltpu.make_async_copy(key_cache.at[at], k_v.at[i % 2], kv_sems.at[0, n]),
            pltpu.make_async_copy(value_cache.at[at], v_v.at[i % 2], kv_sems.at[1, n]),
        )

    caches = [load_kv(n) for n in range(2 * PIECES)]
    for copy in caches[0] + caches[1]:
        copy.start()

    for copy in small:
        copy.wait()
    replies[0].wait()
    for copy in replies[1:]:
        copy.wait_recv()
    slots_of = jnp.transpose(slot_v[...])[:, 0:1]
    picks = lax.broadcasted_iota(jnp.int32, (tokens, owners * SLOTS), 1) == slots_of
    e_own[0:tokens] = jnp.dot(
        picks.astype(jnp.float32).astype(jnp.bfloat16),
        slots_in[...].reshape(owners * SLOTS, features),
        preferred_element_type=jnp.float32,
    ).astype(jnp.bfloat16)
    e_own[tokens:] = gain_v[...]
    e_ring = PairRing(
        e_own,
        lambda i: e_v.at[i],
        lambda i: e_v.at[i, pl.ds(0, tokens // 2)],
        lambda i: e_v.at[i, pl.ds(tokens // 2, tokens // 2 + EXTRA)],
        lambda k, e: p.t_id(e, k),
        lambda k, e: (dp, p.t_id(e, k)),
        e_sems,
    )
    e_ring.s0()
    keep_e = pltpu.make_async_copy(e_own, e_v.at[t], local_sems.at[11])
    keep_e.start()

    def square(ref):
        wide = ref[...].astype(jnp.float32)
        wide = wide * wide
        part = wide[:, 0:LANES]
        for i in range(1, features // LANES):
            part = part + wide[:, i * LANES:(i + 1) * LANES]
        return part

    def add_square(k, e):
        square_v[...] = square_v[...] + square(e_v.at[p.t_id(e, k), pl.ds(0, tokens)])

    cols_a.a.s1()
    cols_a.b.s1()
    square_v[...] = square(e_own.at[pl.ds(0, tokens)])
    e_ring.s1()
    add_square(0, 1)
    cols_a.a.s2()
    cols_a.b.s2()
    e_ring.s2()
    add_square(3, 0)
    add_square(1, 0)
    cols_a.a.s3()
    for copy in first[1]:
        copy.wait_recv()
    cols_b.s0()
    e_ring.s3()
    add_square(3, 1)
    add_square(1, 1)

    part = tensors * height
    loads = {}

    def load_all(cols, ref, into, n, places):
        for k, e in places:
            for dc in (0, 1):
                if dc:
                    cols.took(k, e)
                at = pl.multiple_of(p.dp_id(k, e, dc) * part, part)
                loads[n, k, e, dc] = pltpu.make_async_copy(
                    ref.at[pl.ds(at, part)],
                    into.at[pl.ds(at, part)],
                    load_sems.at[n, dc, k * 2 + e],
                )
                loads[n, k, e, dc].start()

    def loaded(n, places):
        for k, e in places:
            loads[n, k, e, 0].wait()
            loads[n, k, e, 1].wait()

    cols_a.b.s3()
    load_all(cols_a, wa_all, wa_v, 0, AROUND[:6])
    e_ring.s4()
    keep_e.wait()
    add_square(2, 0)
    add_square(2, 1)

    total = jnp.sum(square_v[...], axis=-1, keepdims=True)
    inverse = lax.rsqrt(total / (tensors * features) + EPS)

    def norm(i, carry):
        weight = e_v[i, pl.ds(tokens, EXTRA)].astype(jnp.float32)[0:1]
        normed = e_v[i, pl.ds(0, tokens)].astype(jnp.float32) * inverse * weight
        n_v[i] = normed.astype(jnp.bfloat16)
        return carry

    lax.fori_loop(0, tensors, norm, 0)

    def project(into, w, k, e):
        i = lax.div(p.dp_id(k, e), 2)
        into[...] = into[...] + jnp.dot(
            n_v[i],
            w[pl.ds(pl.multiple_of(i * 2 * part, 2 * part), 2 * part), :],
            preferred_element_type=jnp.float32,
        )

    def project_all(cols, ref, w, into, n):
        def early(j, carry):
            k = lax.div(j, 2)
            project(into, w, jnp.where(k == 2, 3, k), lax.rem(j, 2))
            return carry

        def late(j, carry):
            project(into, w, 2, j)
            return carry

        into[...] = jnp.zeros(into.shape, jnp.float32)
        loaded(n, AROUND[:6])
        lax.fori_loop(0, 6, early, 0)
        cols.a.s4()
        cols.b.s4()
        load_all(cols, ref, w, n, AROUND[6:])
        loaded(n, AROUND[6:])
        lax.fori_loop(0, 2, late, 0)

    cols_b.a.s1()
    cols_b.b.s1()
    project_all(cols_a, wa_all, wa_v, acc_a, 0)
    cols_b.a.s2()
    cols_b.b.s2()

    def placed(raw, head_gain):
        mean_sq = jnp.mean(raw * raw, axis=-1, keepdims=True)
        scaled = raw * lax.rsqrt(mean_sq + EPS) * head_gain
        return scaled * cos_v[...] + pltpu.roll(scaled, width // 2, 1) * sin_v[...]

    head_gain = q_gain[...].astype(jnp.float32)

    def place_heads(acc):
        for h in range(heads // 2):
            at = slice(h * width, (h + 1) * width)
            acc[:, at] = placed(acc[:, at], head_gain)

    place_heads(acc_a)
    nk_v[...] = placed(acc_a[:, hw:hw + kw], k_gain[...].astype(jnp.float32)).astype(jnp.bfloat16)
    nv_v[...] = acc_a[:, hw + kw:hw + 2 * kw].astype(jnp.bfloat16)
    new_keys[...] = nk_v[...]
    new_values[...] = nv_v[...]

    scale = 1.0 / math.sqrt(width)
    pair = 2 * steps
    group = ROWS_AT_ONCE * steps
    some = heads // 2
    query = lax.broadcasted_iota(jnp.int32, (some * pair, 1), 0) % pair
    is_first = query < steps
    fresh = lax.broadcasted_iota(jnp.int32, (some * pair, group), 1)
    column = lax.broadcasted_iota(jnp.int32, (some * pair, cache), 1)

    def attend(acc, half, i, g):
        at = pl.ds(pl.multiple_of(i * piece * steps + g * group, group), group)
        queries = acc[at, 0:hw]
        keys, values = nk_v[at, :], nv_v[at, :]
        results = []
        for n in range(ROWS_AT_ONCE // 2):
            q = jnp.concatenate(
                [
                    queries[n * pair:(n + 1) * pair, h * width:(h + 1) * width]
                    for h in range(some)
                ],
                axis=0,
            ).astype(jnp.bfloat16)
            r = g * ROWS_AT_ONCE + 2 * n
            old_a = lax.dot_general(q, k_v[i % 2, r], NT, preferred_element_type=jnp.float32)
            old_b = lax.dot_general(q, k_v[i % 2, r + 1], NT, preferred_element_type=jnp.float32)
            new = lax.dot_general(q, keys, NT, preferred_element_type=jnp.float32) * scale
            token = query + n * pair
            new = jnp.where((fresh // steps == token // steps) & (fresh <= token), new, -jnp.inf)
            held = jnp.where(
                is_first, lengths[i * piece + r], lengths[i * piece + r + 1]
            )
            old = jnp.where(is_first, old_a, old_b) * scale
            old = jnp.where(column < held, old, -jnp.inf)
            top = jnp.maximum(
                jnp.max(old, axis=-1, keepdims=True), jnp.max(new, axis=-1, keepdims=True)
            )
            old = jnp.exp(old - top)
            new = jnp.exp(new - top)
            whole = jnp.sum(old, axis=-1, keepdims=True) + jnp.sum(new, axis=-1, keepdims=True)
            inv = 1.0 / whole
            old = (old * inv).astype(jnp.bfloat16)
            new = (new * inv).astype(jnp.bfloat16)
            out_a = jnp.dot(old, v_v[i % 2, r], preferred_element_type=jnp.float32)
            out_b = jnp.dot(old, v_v[i % 2, r + 1], preferred_element_type=jnp.float32)
            out = jnp.where(is_first, out_a, out_b)
            out = out + jnp.dot(new, values, preferred_element_type=jnp.float32)
            results.append(
                jnp.concatenate([out[h * pair:(h + 1) * pair] for h in range(some)], axis=1)
            )
        heads_v[half, t, at, :] = jnp.concatenate(results, axis=0).astype(jnp.bfloat16)

    span = tokens // 2

    def heads_ring(kind, half, at, n, sems):
        return kind(
            heads_v.at[half, t, pl.ds(at, n)],
            lambda i: heads_v.at[half, i, pl.ds(at, n)],
            lambda i: heads_v.at[half, i, pl.ds(at, n // 2)],
            lambda i: heads_v.at[half, i, pl.ds(at + n // 2, n // 2)],
            lambda k, e: p.t_id(e, k),
            lambda k, e: (dp, p.t_id(e, k)),
            sems,
        )

    rings = [
        heads_ring(PairRing, 0, 0, tokens, heads_sems.at[0]),
        heads_ring(PairRing, 1, 0, span, heads_sems.at[1]),
        heads_ring(RingPair, 1, span, span, heads_sems.at[2]),
    ]

    def attend_piece(acc, half, i):
        n = half * PIECES + i
        for copy in caches[n]:
            copy.wait()

        def one(g, carry):
            attend(acc, half, i, g)
            return carry

        lax.fori_loop(0, piece // ROWS_AT_ONCE, one, 0)
        if n + 2 < 2 * PIECES:
            for copy in caches[n + 2]:
                copy.start()

    attend_piece(acc_a, 0, 0)
    cols_b.a.s3()
    for copy in second:
        copy.wait_recv()
    outs.s0()
    keep_o = pltpu.make_async_copy(wo_part, wo_v.at[pl.ds(dp * tensors, tensors)], local_sems.at[12])
    keep_o.start()
    attend_piece(acc_a, 0, 1)
    cols_b.b.s3()
    load_all(cols_b, wb_all, wb_v, 1, AROUND[:6])
    attend_piece(acc_a, 0, 2)
    attend_piece(acc_a, 0, 3)
    rings[0].s0()
    project_all(cols_b, wb_all, wb_v, acc_b, 1)
    outs.a.s1()
    rings[0].s1()
    place_heads(acc_b)
    outs.b.s1()
    attend_piece(acc_b, 1, 0)
    rings[0].s2()
    outs.a.s2()
    attend_piece(acc_b, 1, 1)
    rings[1].s0()
    outs.b.s2()
    rings[0].s3()
    attend_piece(acc_b, 1, 2)
    outs.a.s3()
    rings[1].s1()
    attend_piece(acc_b, 1, 3)
    rings[2].s0()
    rings[1].s2()
    rings[2].s1()
    outs.b.s3()
    rings[1].s3()
    rings[2].s2()
    rings[0].s4()
    outs.a.s4()
    outs.b.s4()
    for k, e in AROUND:
        outs.took(k, e)
    keep_o.wait()

    per = wo_v.shape[0] // tensors // 2
    total_v[...] = e_own[pl.ds(0, tokens)].astype(jnp.float32)

    def back(half):
        def add(i, carry):
            w = wo_v[pl.ds((2 * i + half) * per, per)].reshape(hw, ow)
            total_v[...] = total_v[...] + jnp.dot(
                heads_v[half, i], w, preferred_element_type=jnp.float32
            )
            return carry

        lax.fori_loop(0, tensors, add, 0)

    back(0)
    rings[1].s4()
    rings[2].s3()
    rings[2].s4()
    back(1)
    attended[...] = total_v[...].astype(jnp.bfloat16)
    for copy in first[0] + first[1] + asks + replies[1:] + second:
        copy.wait_send()
    cols_a.end()
    cols_b.end()
    outs.end()
    e_ring.end()
    for ring in rings:
        ring.end()


def step(lengths, req, slot, gain, table, wq, wk, wv, wo, q_gain, k_gain, cosine, sine, keys, values):
    owners, tensors = lax.axis_size("dp"), lax.axis_size("tensor")
    tokens, features = slot.shape[1], table.shape[1]
    rows, cache, width = keys.shape
    height, depth = wq.shape[0], wo.shape[0]
    qw, ow = wq.shape[1] // tensors, wo.shape[1] // tensors
    hw = qw // 2
    piece = rows // PIECES
    anywhere, vmem = pl.BlockSpec(memory_space=pl.ANY), pl.BlockSpec(memory_space=pltpu.VMEM)
    smem = pl.BlockSpec(memory_space=pltpu.SMEM)
    dma = pltpu.SemaphoreType.DMA
    bf16, f32 = jnp.bfloat16, jnp.float32
    return pl.pallas_call(
        step_kernel,
        out_shape=(
            jax.ShapeDtypeStruct((tokens, ow), bf16),
            jax.ShapeDtypeStruct((tokens, width), bf16),
            jax.ShapeDtypeStruct((tokens, width), bf16),
            jax.ShapeDtypeStruct((1, 1), jnp.int32),
            jax.ShapeDtypeStruct((owners * tensors * height, hw + 2 * width), bf16),
            jax.ShapeDtypeStruct((owners * tensors * height, hw), bf16),
        ),
        in_specs=[smem] + [anywhere] * 8 + [vmem] * 2 + [anywhere] * 4,
        out_specs=(vmem, vmem, vmem, smem, anywhere, anywhere),
        scratch_shapes=[
            pltpu.VMEM((owners, 8, LANES), jnp.int32),
            pltpu.VMEM(slot.shape, jnp.int32),
            pltpu.VMEM(gain.shape, bf16),
            pltpu.VMEM(cosine.shape, f32),
            pltpu.VMEM(sine.shape, f32),
            pltpu.VMEM((owners * SLOTS, LANES), jnp.int32),
            pltpu.VMEM((owners, SLOTS, features), bf16),
            pltpu.VMEM((owners, SLOTS, features), bf16),
            pltpu.VMEM((tokens + EXTRA, features), bf16),
            pltpu.VMEM((tensors, tokens + EXTRA, features), bf16),
            pltpu.VMEM((tensors, tokens, features), bf16),
            pltpu.VMEM((tokens, LANES), f32),
            pltpu.VMEM((tensors * features, hw + 2 * width), bf16),
            pltpu.VMEM((tensors * features, hw), bf16),
            pltpu.VMEM((tensors, depth, ow), bf16),
            pltpu.VMEM((owners * tensors, depth, ow), bf16),
            pltpu.VMEM((2, tensors, tokens, hw), bf16),
            pltpu.VMEM((tokens, hw + 2 * width), f32),
            pltpu.VMEM((tokens, hw), f32),
            pltpu.VMEM((tokens, width), bf16),
            pltpu.VMEM((tokens, width), bf16),
            pltpu.VMEM((2, piece, cache, width), bf16),
            pltpu.VMEM((2, piece, cache, width), bf16),
            pltpu.VMEM((tokens, ow), f32),
            dma((2, owners)),
            dma((2, owners)),
            dma((2, 4 * tensors)),
            dma((2, tensors)),
            dma((3, 2, 2, PairRing.COPIES)),
            dma((3, 2, 2, CoreShare.COPIES)),
            dma((2, PairRing.COPIES)),
            dma((3, 2, PairRing.COPIES)),
            dma((2, 2, 8)),
            dma((2, 2 * PIECES)),
            dma((17,)),
        ],
        compiler_params=pltpu.CompilerParams(
            collective_id=1, has_side_effects=True, vmem_limit_bytes=60 * 1024 * 1024
        ),
        name="step",
    )(lengths, req, slot, gain, table, wq, wk, wv, wo, q_gain, k_gain, cosine, sine, keys, values)


def requests(ids, vocab_rows, owners):
    count = ids.shape[0]
    owner = lax.div(ids, jnp.int32(vocab_rows))
    same = ids[:, None] == ids[None, :]
    before = jnp.arange(count)[None, :] < jnp.arange(count)[:, None]
    fresh = ~jnp.any(same & before, axis=1)
    smaller = (owner[:, None] == owner[None, :]) & (ids[None, :] < ids[:, None])
    rank = jnp.sum(smaller & fresh[None, :], axis=1, dtype=jnp.int32)
    over = jnp.any(rank >= SLOTS).astype(jnp.int32)
    mine = (owner[None, None, :] == jnp.arange(owners)[:, None, None]) & (
        rank[None, None, :] == jnp.arange(SLOTS)[None, :, None]
    )
    wanted = jnp.max(jnp.where(mine, (ids - owner * vocab_rows)[None, None, :], -1), axis=-1)
    rest = jnp.full((owners, LANES - SLOTS), over, jnp.int32)
    asked = jnp.concatenate([wanted, rest], axis=1)
    req = jnp.broadcast_to(asked[:, None, :], (owners, 8, LANES))
    return req, jnp.broadcast_to((owner * SLOTS + rank)[None, :], (8, count))


def rms_scale(values, gain):
    mean_sq = jnp.mean(values * values, axis=-1, keepdims=True)
    return values * lax.rsqrt(mean_sq + EPS) * gain.astype(jnp.float32)


def rotate(values, positions):
    half = values.shape[-1] // 2
    freq = THETA ** (-jnp.arange(half, dtype=jnp.float32) * 2.0 / values.shape[-1])
    angle = positions.astype(jnp.float32)[:, :, None, None] * freq
    cosine = jnp.cos(angle)
    sine = jnp.sin(angle)
    first = values[..., :half]
    second = values[..., half:]
    return jnp.concatenate(
        [first * cosine - second * sine, second * cosine + first * sine], axis=-1
    )


def attend(query, fresh_keys, fresh_values, key_cache, value_cache, lengths):
    rows, steps, heads_count, width = query.shape
    kv_heads = fresh_keys.shape[2]
    group = heads_count // kv_heads
    cache_len = key_cache.shape[1]
    grouped = query.reshape(rows, steps, kv_heads, group, width)
    keys = key_cache.reshape(rows, cache_len, kv_heads, width)
    values = value_cache.reshape(rows, cache_len, kv_heads, width)
    scale = 1.0 / math.sqrt(width)
    old_scores = (
        jnp.einsum("rskgd,rckd->rkgsc", grouped, keys, preferred_element_type=jnp.float32) * scale
    )
    new_scores = (
        jnp.einsum("rskgd,rtkd->rkgst", grouped, fresh_keys, preferred_element_type=jnp.float32)
        * scale
    )
    valid = jnp.arange(cache_len)[None, :] < lengths[:, None]
    old_scores = jnp.where(valid[:, None, None, None, :], old_scores, -jnp.inf)
    causal = jnp.arange(steps)[None, :] <= jnp.arange(steps)[:, None]
    new_scores = jnp.where(causal[None, None, None, :, :], new_scores, -jnp.inf)
    highest = jnp.maximum(jnp.max(old_scores, axis=-1), jnp.max(new_scores, axis=-1))
    old_exp = jnp.exp(old_scores - highest[..., None])
    new_exp = jnp.exp(new_scores - highest[..., None])
    total = jnp.sum(old_exp, axis=-1) + jnp.sum(new_exp, axis=-1)
    old_weights = (old_exp / total[..., None]).astype(jnp.bfloat16)
    new_weights = (new_exp / total[..., None]).astype(jnp.bfloat16)
    mixed = jnp.einsum("rkgsc,rckd->rskgd", old_weights, values, preferred_element_type=jnp.float32)
    mixed = mixed + jnp.einsum(
        "rkgst,rtkd->rskgd", new_weights, fresh_values, preferred_element_type=jnp.float32
    )
    return mixed.reshape(rows, steps, heads_count * width).astype(jnp.bfloat16)


def owned_columns(local):
    half = lax.all_to_all(local, "tensor", split_axis=1, concat_axis=0, tiled=True)
    return lax.all_gather(half, "dp", axis=0, tiled=True)


def plain(
    token_ids, lengths, embed_table, norm_gain, w_query, w_key, w_value, w_out, q_gain, k_gain, key_cache, value_cache
):
    rows, steps = token_ids.shape
    width = q_gain.shape[0]
    every_id = lax.all_gather(token_ids, "dp", axis=0, tiled=True)
    vocab_rows = embed_table.shape[0]
    local_id = every_id - lax.axis_index("dp") * vocab_rows
    inside = (local_id >= 0) & (local_id < vocab_rows)
    picked = jnp.take(embed_table, jnp.clip(local_id, 0, vocab_rows - 1), axis=0)
    partial_rows = jnp.where(inside[..., None], picked, jnp.zeros((), jnp.bfloat16))
    own_rows = lax.psum_scatter(partial_rows, "dp", scatter_dimension=0, tiled=True)
    whole = lax.all_gather(own_rows, "tensor", axis=2, tiled=True)
    gain_full = lax.all_gather(norm_gain, "tensor", axis=0, tiled=True)
    normed = rms_scale(whole.astype(jnp.float32), gain_full).astype(jnp.bfloat16)
    flat = normed.reshape(rows * steps, -1)
    wq = owned_columns(w_query)
    wk = owned_columns(w_key)
    wv = owned_columns(w_value)
    wo = owned_columns(w_out)
    query_raw = jnp.dot(flat, wq, preferred_element_type=jnp.float32)
    key_raw = jnp.dot(flat, wk, preferred_element_type=jnp.float32)
    value_raw = jnp.dot(flat, wv, preferred_element_type=jnp.float32)
    positions = lengths[:, None] + jnp.arange(steps, dtype=jnp.int32)[None, :]
    query_raw = query_raw.reshape(rows, steps, -1, width)
    key_raw = key_raw.reshape(rows, steps, -1, width)
    fresh_values = value_raw.astype(jnp.bfloat16).reshape(rows, steps, -1, width)
    query = rotate(rms_scale(query_raw, q_gain), positions).astype(jnp.bfloat16)
    fresh_keys = rotate(rms_scale(key_raw, k_gain), positions).astype(jnp.bfloat16)
    local_heads = attend(query, fresh_keys, fresh_values, key_cache, value_cache, lengths)
    all_heads = lax.all_gather(local_heads, "tensor", axis=2, tiled=True).reshape(rows * steps, -1)
    projected = jnp.dot(all_heads, wo, preferred_element_type=jnp.float32)
    output = projected + own_rows.astype(jnp.float32).reshape(rows * steps, -1)
    attended = output.astype(jnp.bfloat16).reshape(rows, steps, -1)
    return (attended, fresh_keys.reshape(rows, steps, -1), fresh_values.reshape(rows, steps, -1))


def shards(
    token_ids,
    lengths,
    embed_table,
    norm_gain,
    w_query,
    w_key,
    w_value,
    w_out,
    q_gain,
    k_gain,
    key_cache,
    value_cache,
):
    owners = lax.axis_size("dp")
    rows, steps = token_ids.shape
    width = q_gain.shape[0]
    req, slot = requests(token_ids.reshape(-1), embed_table.shape[0], owners)
    positions = lengths[:, None] + jnp.arange(steps, dtype=jnp.int32)[None, :]
    half = width // 2
    freq = THETA ** (-(np.arange(width) % half) * 2.0 / width)
    angle = positions.astype(jnp.float32)[:, :, None] * freq.astype(np.float32)
    sign = np.where(np.arange(width) < half, -1.0, 1.0).astype(np.float32)
    cosine = jnp.cos(angle).reshape(rows * steps, width)
    sine = (jnp.sin(angle) * sign).reshape(rows * steps, width)
    attended, new_keys, new_values, flag, _, _ = step(
        lengths, req, slot, jnp.broadcast_to(norm_gain[None], (EXTRA, norm_gain.shape[0])), embed_table, w_query, w_key, w_value, w_out,
        q_gain[None], k_gain[None], cosine, sine, key_cache, value_cache,
    )
    given = (
        token_ids, lengths, embed_table, norm_gain, w_query, w_key, w_value, w_out, q_gain, k_gain,
        key_cache, value_cache,
    )
    return lax.cond(
        flag[0, 0] > 0,
        lambda: plain(*given),
        lambda: (
            attended.reshape(rows, steps, -1),
            new_keys.reshape(rows, steps, -1),
            new_values.reshape(rows, steps, -1),
        ),
    )


def solution(mesh):
    in_specs = (
        P("dp", None),
        P("dp"),
        P("dp", "tensor"),
        P("tensor"),
        P(("dp", "tensor"), None),
        P(("dp", "tensor"), None),
        P(("dp", "tensor"), None),
        P(("dp", "tensor"), None),
        P(),
        P(),
        P("dp", None, "tensor"),
        P("dp", None, "tensor"),
    )
    out_specs = (P("dp", None, "tensor"), P("dp", None, "tensor"), P("dp", None, "tensor"))
    return jax.shard_map(shards, mesh=mesh, in_specs=in_specs, out_specs=out_specs, check_vma=False)
```

time: 650 us -> 177 us (0.27); the launches traced: 638 us -> 176 us
  waiting for transfers between devices: 328 us -> 0 us
  Pallas kernels: 0 us -> 149 us
  blocking collectives: 124 us -> 0 us
  local copies, waits for them, and re-layouts: 77.2 us -> 7.45 us
  starting transfers between devices: 38.9 us -> 0 us
  matrix products: 28.7 us -> 0 us
  other arithmetic: 27 us -> 4.07 us
    pallas_call x0 -> x1, Pallas kernels: none -> 149 us  [step(): pl.pallas_call(step_kernel, out_shape=(jax.ShapeDtypeStruct((tokens, ow),...]
    all_gather x2 -> x0, waiting for transfers between devices: 140 us -> none  [the longest x1 140 us: shards(): lax.all_gather(local_heads, 'tensor', axis=2, tiled=True)]
    all_gather x2 -> x0, blocking collectives: 124 us -> none  [the longest x1 97.5 us: shards(): lax.all_gather(norm_gain, 'tensor', axis=0, tiled=True)]
    unnamed x4 -> x0, waiting for transfers between devices: 118 us -> none
    all_to_all x4 -> x0, waiting for transfers between devices: 69.4 us -> none  [the longest x1 35.2 us: shards(): lax.all_to_all(spread(w_key, replicas, owners), ('dp', 'tensor'), split_a...]
    all_to_all x4 -> x0, starting transfers between devices: 38.5 us -> none  [the longest x1 17.3 us: shards(): lax.all_to_all(spread(w_out, replicas, owners), ('dp', 'tensor'), split_a...]
    gather x2 -> x0, local copies, waits for them, and re-layouts: 31.1 us -> none  [shards(): jnp.take(embed_table, jnp.clip(local_id, 0, vocab_rows - 1), axis=0)]
    dot_general x8 -> x0, matrix products: 28.7 us -> none  [the longest x1 8.71 us: shards(): jnp.dot(all_heads, out_local, preferred_element_type=jnp.float32)]
  transfers between devices with their start and end apart: 7 -> 0, of which waited for: 4 -> 0; matrix products, arithmetic and copies ran while one was open for 12% -> 0% of each run, Pallas kernels for 0% -> 0%
where the time goes in v2:
time: 177 us; the launch traced here: 176 us
  Pallas kernels  149 us (84%)
  between operations  15.4 us (9%)
  local copies, waits for them, and re-layouts  7.45 us (4%)
  other arithmetic  4.07 us (2%)
    pallas_call x1, Pallas kernels, step(): pl.pallas_call(step_kernel, out_shape=(jax.ShapeDtypeStruct((tokens, ow),...  149 us

profile of v2, /device:TPU:1, one launch (start us, length us, event | category | flops | bytes accessed | tf_op | source)
XLA Modules:
  0.0 176.2 jit_solution(1336896655354739382)
XLA Ops:
  7.2 0.8 copy.109
  7.9 0.1 reshape.404
  8.1 0.2 fusion.47
  8.3 0.2 convert_reduce_fusion
  8.5 0.3 select_reduce_fusion
  8.9 0.6 compare_reduce_fusion
  10.2 0.6 broadcast_in_dim.64.req
  10.8 0.6 broadcast_in_dim.65.slot
  11.4 0.7 add_convert_fusion.2
  12.1 0.1 convert_element_type.82
  12.2 1.9 %fusion.48 = (f32[256,128]{1,0:T(8,128)}, f32[256,128]{1,0:T(8,128)}) fusion(f32[128]{0:T(128)} %constant.74.clone, f32[128]{0:T(128)} %constant.73.clone, f32[256]{0:T(256)S(1)} %convert_element_type.82), kind=kLoop, calls=%fused_computation.91 | loop fusion | flops 65536 | bytes 264192 | tf_op jit(solution)/shard_map/mul | solution.py:911
  14.2 1.3 broadcast_in_dim.66.gain
  15.5 0.0 copy-start.10
  15.5 0.0 copy-start.11
  15.5 0.0 copy-start.12
  15.5 0.0 copy-start.13
  15.5 149.0 %step.1 = (bf16[256,640]{1,0:T(8,128)(2,1)}, bf16[256,128]{1,0:T(8,128)(2,1)}, bf16[256,128]{1,0:T(8,128)(2,1)S(1)}, s32[1,1]{1,0:T(1,128)}, bf16[5120,768]{1,0:T(8,128)(2,1)}, /*index=5*/bf16[5120,512]{1,0:T(8,128)(2,1)}) custom-call(s32[64]{0:T(128)} %lengths.1, s32[16,8,128]{2,1,0:T(8,128)} %broadcast_in_dim.64.req, s32[8,256]{1,0:T(8,128)} %broadcast_in_dim.65.slot, ...), custom_call_target="tpu_custom_call" | custom-call | tf_op jit(solution)/shard_map/step/pallas_call | solution.py:719
  165.1 0.0 copy-done.2
  165.1 0.0 copy-done.5
  165.1 0.0 copy-done.6
  165.2 0.3 conditional.1
  165.5 1.8 %reshape.406 = bf16[64,4,640]{2,1,0:T(4,128)(2,1)} reshape(bf16[256,640]{1,0:T(8,128)(2,1)} %get-tuple-element.57) | data formatting | bytes 655360 | tf_op jit(solution)/shard_map/cond/branch_0_fun/reshape | solution.py:924
  167.2 1.5 copy.155
  168.7 0.6 copy.156
  (15 shorter events, 0.1 us)
Async XLA Ops:
  15.4 149.7 %copy-start.2 = (bf16[40,8192]{1,0:T(8,128)(2,1)S(1)}, bf16[40,8192]{1,0:T(8,128)(2,1)}, u32[]{:S(2)}) copy-start(bf16[40,8192]{1,0:T(8,128)(2,1)} %wq.1) | copy-start | bytes 1966084
  15.4 149.7 %copy-start.5 = (bf16[40,1024]{1,0:T(8,128)(2,1)S(1)}, bf16[40,1024]{1,0:T(8,128)(2,1)}, u32[]{:S(2)}) copy-start(bf16[40,1024]{1,0:T(8,128)(2,1)} %wk.1) | copy-start | bytes 245764
  15.4 149.7 %copy-start.6 = (bf16[40,1024]{1,0:T(8,128)(2,1)S(1)}, bf16[40,1024]{1,0:T(8,128)(2,1)}, u32[]{:S(2)}) copy-start(bf16[40,1024]{1,0:T(8,128)(2,1)} %wv.1) | copy-start | bytes 245764
  15.4 149.7 %copy-start.9 = (s32[64]{0:T(128)S(1)}, s32[64]{0:T(128)}, u32[]{:S(2)}) copy-start(s32[64]{0:T(128)} %lengths.1) | copy-start | bytes 772
  15.5 149.7 %copy-start.10 = (s32[64,4]{0,1:T(4,128)S(1)}, s32[64,4]{0,1:T(4,128)}, u32[]{:S(2)}) copy-start(s32[64,4]{0,1:T(4,128)} %param.16) | copy-start | bytes 3076
  15.5 149.7 %copy-start.11 = (bf16[640]{0:T(1024)(128)(2,1)S(1)}, bf16[640]{0:T(1024)(128)(2,1)}, u32[]{:S(2)}) copy-start(bf16[640]{0:T(1024)(128)(2,1)} %param.19) | copy-start | bytes 3844
  15.5 149.7 %copy-start.12 = (bf16[128]{0:T(256)(128)(2,1)S(1)}, bf16[128]{0:T(256)(128)(2,1)}, u32[]{:S(2)}) copy-start(bf16[128]{0:T(256)(128)(2,1)} %param.24) | copy-start | bytes 772
  15.5 149.7 %copy-start.13 = (bf16[128]{0:T(256)(128)(2,1)S(1)}, bf16[128]{0:T(256)(128)(2,1)}, u32[]{:S(2)}) copy-start(bf16[128]{0:T(256)(128)(2,1)} %param.25) | copy-start | bytes 772

commit v3 on v2

--- a/solution.py
+++ b/solution.py
@@ -10,7 +10,7 @@
 
 EPS = 1e-06
 THETA = 1000000.0
-ROWS_AT_ONCE = 4
+ROWS_AT_ONCE = 8
 PIECES = 4
 SLOTS = 32
 LANES = 128
@@ -553,17 +553,22 @@
     pair = 2 * steps
     group = ROWS_AT_ONCE * steps
     some = heads // 2
-    query = lax.broadcasted_iota(jnp.int32, (some * pair, 1), 0) % pair
-    is_first = query < steps
-    fresh = lax.broadcasted_iota(jnp.int32, (some * pair, group), 1)
-    column = lax.broadcasted_iota(jnp.int32, (some * pair, cache), 1)
+    count = ROWS_AT_ONCE // 2
+    each = some * pair
+    index = lax.broadcasted_iota(jnp.int32, (count * each, 1), 0)
+    token = index // each * pair + index % pair
+    is_first = lax.broadcasted_iota(jnp.int32, (each, 1), 0) % pair < steps
+    fresh = lax.broadcasted_iota(jnp.int32, (count * each, group), 1)
+    seen = (fresh // steps == token // steps) & (fresh <= token)
+    column = lax.broadcasted_iota(jnp.int32, (count * each, cache), 1)
+    none = jnp.zeros((each, width), jnp.bfloat16)
 
     def attend(acc, half, i, g):
         at = pl.ds(pl.multiple_of(i * piece * steps + g * group, group), group)
         queries = acc[at, 0:hw]
         keys, values = nk_v[at, :], nv_v[at, :]
-        results = []
-        for n in range(ROWS_AT_ONCE // 2):
+        parts, scores, held = [], [], []
+        for n in range(count):
             q = jnp.concatenate(
                 [
                     queries[n * pair:(n + 1) * pair, h * width:(h + 1) * width]
@@ -571,30 +576,41 @@
                 ],
                 axis=0,
             ).astype(jnp.bfloat16)
+            parts.append(q)
             r = g * ROWS_AT_ONCE + 2 * n
-            old_a = lax.dot_general(q, k_v[i % 2, r], NT, preferred_element_type=jnp.float32)
-            old_b = lax.dot_general(q, k_v[i % 2, r + 1], NT, preferred_element_type=jnp.float32)
-            new = lax.dot_general(q, keys, NT, preferred_element_type=jnp.float32) * scale
-            token = query + n * pair
-            new = jnp.where((fresh // steps == token // steps) & (fresh <= token), new, -jnp.inf)
-            held = jnp.where(
-                is_first, lengths[i * piece + r], lengths[i * piece + r + 1]
+            wide_q = jnp.concatenate(
+                [jnp.where(is_first, q, none), jnp.where(is_first, none, q)], axis=1
             )
-            old = jnp.where(is_first, old_a, old_b) * scale
-            old = jnp.where(column < held, old, -jnp.inf)
-            top = jnp.maximum(
-                jnp.max(old, axis=-1, keepdims=True), jnp.max(new, axis=-1, keepdims=True)
+            both_k = jnp.concatenate([k_v[i % 2, r], k_v[i % 2, r + 1]], axis=1)
+            scores.append(
+                lax.dot_general(wide_q, both_k, NT, preferred_element_type=jnp.float32)
             )
-            old = jnp.exp(old - top)
-            new = jnp.exp(new - top)
-            whole = jnp.sum(old, axis=-1, keepdims=True) + jnp.sum(new, axis=-1, keepdims=True)
-            inv = 1.0 / whole
-            old = (old * inv).astype(jnp.bfloat16)
-            new = (new * inv).astype(jnp.bfloat16)
-            out_a = jnp.dot(old, v_v[i % 2, r], preferred_element_type=jnp.float32)
-            out_b = jnp.dot(old, v_v[i % 2, r + 1], preferred_element_type=jnp.float32)
-            out = jnp.where(is_first, out_a, out_b)
-            out = out + jnp.dot(new, values, preferred_element_type=jnp.float32)
+            held.append(
+                jnp.where(is_first, lengths[i * piece + r], lengths[i * piece + r + 1])
+            )
+        new = lax.dot_general(
+            jnp.concatenate(parts, axis=0), keys, NT, preferred_element_type=jnp.float32
+        )
+        new = jnp.where(seen, new * scale, -jnp.inf)
+        old = jnp.concatenate(scores, axis=0) * scale
+        old = jnp.where(column < jnp.concatenate(held, axis=0), old, -jnp.inf)
+        top = jnp.maximum(
+            jnp.max(old, axis=-1, keepdims=True), jnp.max(new, axis=-1, keepdims=True)
+        )
+        old = jnp.exp(old - top)
+        new = jnp.exp(new - top)
+        whole = jnp.sum(old, axis=-1, keepdims=True) + jnp.sum(new, axis=-1, keepdims=True)
+        inv = 1.0 / whole
+        old = (old * inv).astype(jnp.bfloat16)
+        new = (new * inv).astype(jnp.bfloat16)
+        out_new = jnp.dot(new, values, preferred_element_type=jnp.float32)
+        results = []
+        for n in range(count):
+            r = g * ROWS_AT_ONCE + 2 * n
+            both_v = jnp.concatenate([v_v[i % 2, r], v_v[i % 2, r + 1]], axis=1)
+            mine = slice(n * each, (n + 1) * each)
+            both = jnp.dot(old[mine], both_v, preferred_element_type=jnp.float32)
+            out = jnp.where(is_first, both[:, :width], both[:, width:]) + out_new[mine]
             results.append(
                 jnp.concatenate([out[h * pair:(h + 1) * pair] for h in range(some)], axis=1)
             )

time: 177 us -> 172 us (0.972)
  Pallas kernels: 149 us -> 144 us
    pallas_call x1, Pallas kernels: 149 us -> 144 us  [step(): pl.pallas_call(step_kernel, out_shape=(jax.ShapeDtypeStruct((tokens, ow),...]
where the time goes in v3:
time: 172 us; the launch traced here: 171 us
  Pallas kernels  144 us (84%)
  between operations  15.4 us (9%)
  local copies, waits for them, and re-layouts  7.45 us (4%)
  other arithmetic  4.07 us (2%)
    pallas_call x1, Pallas kernels, step(): pl.pallas_call(step_kernel, out_shape=(jax.ShapeDtypeStruct((tokens, ow),...  144 us

profile of v3, /device:TPU:1, one launch (start us, length us, event | category | flops | bytes accessed | tf_op | source)
XLA Modules:
  0.0 171.2 jit_solution(6422932135594568695)
XLA Ops:
  7.2 0.8 copy.109
  7.9 0.1 reshape.404
  8.1 0.2 fusion.47
  8.3 0.2 convert_reduce_fusion
  8.5 0.3 select_reduce_fusion
  8.9 0.6 compare_reduce_fusion
  10.2 0.6 broadcast_in_dim.64.req
  10.8 0.6 broadcast_in_dim.65.slot
  11.4 0.7 add_convert_fusion.2
  12.1 0.1 convert_element_type.82
  12.2 1.9 %fusion.48 = (f32[256,128]{1,0:T(8,128)}, f32[256,128]{1,0:T(8,128)}) fusion(f32[128]{0:T(128)} %constant.74.clone, f32[128]{0:T(128)} %constant.73.clone, f32[256]{0:T(256)S(1)} %convert_element_type.82), kind=kLoop, calls=%fused_computation.91 | loop fusion | flops 65536 | bytes 264192 | tf_op jit(solution)/shard_map/mul | solution.py:927
  14.2 1.3 broadcast_in_dim.66.gain
  15.5 0.0 copy-start.10
  15.5 0.0 copy-start.11
  15.5 0.0 copy-start.12
  15.5 0.0 copy-start.13
  15.5 144.0 %step.1 = (bf16[256,640]{1,0:T(8,128)(2,1)}, bf16[256,128]{1,0:T(8,128)(2,1)}, bf16[256,128]{1,0:T(8,128)(2,1)S(1)}, s32[1,1]{1,0:T(1,128)}, bf16[5120,768]{1,0:T(8,128)(2,1)}, /*index=5*/bf16[5120,512]{1,0:T(8,128)(2,1)}) custom-call(s32[64]{0:T(128)} %lengths.1, s32[16,8,128]{2,1,0:T(8,128)} %broadcast_in_dim.64.req, s32[8,256]{1,0:T(8,128)} %broadcast_in_dim.65.slot, ...), custom_call_target="tpu_custom_call" | custom-call | tf_op jit(solution)/shard_map/step/pallas_call | solution.py:735
  160.0 0.0 copy-done.2
  160.0 0.0 copy-done.5
  160.1 0.0 copy-done.6
  160.1 0.3 conditional.1
  160.4 1.8 %reshape.406 = bf16[64,4,640]{2,1,0:T(4,128)(2,1)} reshape(bf16[256,640]{1,0:T(8,128)(2,1)} %get-tuple-element.57) | data formatting | bytes 655360 | tf_op jit(solution)/shard_map/cond/branch_0_fun/reshape | solution.py:940
  162.2 1.5 copy.155
  163.7 0.6 copy.156
  (15 shorter events, 0.1 us)
Async XLA Ops:
  15.4 144.6 %copy-start.2 = (bf16[40,8192]{1,0:T(8,128)(2,1)S(1)}, bf16[40,8192]{1,0:T(8,128)(2,1)}, u32[]{:S(2)}) copy-start(bf16[40,8192]{1,0:T(8,128)(2,1)} %wq.1) | copy-start | bytes 1966084
  15.4 144.6 %copy-start.5 = (bf16[40,1024]{1,0:T(8,128)(2,1)S(1)}, bf16[40,1024]{1,0:T(8,128)(2,1)}, u32[]{:S(2)}) copy-start(bf16[40,1024]{1,0:T(8,128)(2,1)} %wk.1) | copy-start | bytes 245764
  15.4 144.6 %copy-start.6 = (bf16[40,1024]{1,0:T(8,128)(2,1)S(1)}, bf16[40,1024]{1,0:T(8,128)(2,1)}, u32[]{:S(2)}) copy-start(bf16[40,1024]{1,0:T(8,128)(2,1)} %wv.1) | copy-start | bytes 245764
  15.4 144.6 %copy-start.9 = (s32[64]{0:T(128)S(1)}, s32[64]{0:T(128)}, u32[]{:S(2)}) copy-start(s32[64]{0:T(128)} %lengths.1) | copy-start | bytes 772
  15.5 144.6 %copy-start.10 = (s32[64,4]{0,1:T(4,128)S(1)}, s32[64,4]{0,1:T(4,128)}, u32[]{:S(2)}) copy-start(s32[64,4]{0,1:T(4,128)} %param.16) | copy-start | bytes 3076
  15.5 144.6 %copy-start.11 = (bf16[640]{0:T(1024)(128)(2,1)S(1)}, bf16[640]{0:T(1024)(128)(2,1)}, u32[]{:S(2)}) copy-start(bf16[640]{0:T(1024)(128)(2,1)} %param.19) | copy-start | bytes 3844
  15.5 144.6 %copy-start.12 = (bf16[128]{0:T(256)(128)(2,1)S(1)}, bf16[128]{0:T(256)(128)(2,1)}, u32[]{:S(2)}) copy-start(bf16[128]{0:T(256)(128)(2,1)} %param.24) | copy-start | bytes 772
  15.5 144.6 %copy-start.13 = (bf16[128]{0:T(256)(128)(2,1)S(1)}, bf16[128]{0:T(256)(128)(2,1)}, u32[]{:S(2)}) copy-start(bf16[128]{0:T(256)(128)(2,1)} %param.25) | copy-start | bytes 772

commit v4 on v3

--- a/solution.py
+++ b/solution.py
@@ -651,13 +651,13 @@
 
     attend_piece(acc_a, 0, 0)
     cols_b.a.s3()
+    attend_piece(acc_a, 0, 1)
+    cols_b.b.s3()
     for copy in second:
         copy.wait_recv()
     outs.s0()
     keep_o = pltpu.make_async_copy(wo_part, wo_v.at[pl.ds(dp * tensors, tensors)], local_sems.at[12])
     keep_o.start()
-    attend_piece(acc_a, 0, 1)
-    cols_b.b.s3()
     load_all(cols_b, wb_all, wb_v, 1, AROUND[:6])
     attend_piece(acc_a, 0, 2)
     attend_piece(acc_a, 0, 3)

time: 172 us -> 173 us (level)
  Pallas kernels: 144 us -> 146 us
    pallas_call x1, Pallas kernels: 144 us -> 146 us  [step(): pl.pallas_call(step_kernel, out_shape=(jax.ShapeDtypeStruct((tokens, ow),...]
where the time goes in v4:
time: 173 us
  Pallas kernels  146 us (84%)
  between operations  15.4 us (9%)
  local copies, waits for them, and re-layouts  7.45 us (4%)
  other arithmetic  4.07 us (2%)
    pallas_call x1, Pallas kernels, step(): pl.pallas_call(step_kernel, out_shape=(jax.ShapeDtypeStruct((tokens, ow),...  146 us

profile of v4, /device:TPU:1, one launch (start us, length us, event | category | flops | bytes accessed | tf_op | source)
XLA Modules:
  0.0 173.0 jit_solution(17857827173820377597)
XLA Ops:
  7.2 0.8 copy.109
  7.9 0.1 reshape.404
  8.1 0.2 fusion.47
  8.3 0.2 convert_reduce_fusion
  8.5 0.3 select_reduce_fusion
  8.9 0.6 compare_reduce_fusion
  10.2 0.6 broadcast_in_dim.64.req
  10.8 0.6 broadcast_in_dim.65.slot
  11.4 0.7 add_convert_fusion.2
  12.1 0.1 convert_element_type.82
  12.2 1.9 %fusion.48 = (f32[256,128]{1,0:T(8,128)}, f32[256,128]{1,0:T(8,128)}) fusion(f32[128]{0:T(128)} %constant.74.clone, f32[128]{0:T(128)} %constant.73.clone, f32[256]{0:T(256)S(1)} %convert_element_type.82), kind=kLoop, calls=%fused_computation.91 | loop fusion | flops 65536 | bytes 264192 | tf_op jit(solution)/shard_map/mul | solution.py:927
  14.2 1.3 broadcast_in_dim.66.gain
  15.5 0.0 copy-start.10
  15.5 0.0 copy-start.11
  15.5 0.0 copy-start.12
  15.5 0.0 copy-start.13
  15.5 145.8 %step.1 = (bf16[256,640]{1,0:T(8,128)(2,1)}, bf16[256,128]{1,0:T(8,128)(2,1)}, bf16[256,128]{1,0:T(8,128)(2,1)S(1)}, s32[1,1]{1,0:T(1,128)}, bf16[5120,768]{1,0:T(8,128)(2,1)}, /*index=5*/bf16[5120,512]{1,0:T(8,128)(2,1)}) custom-call(s32[64]{0:T(128)} %lengths.1, s32[16,8,128]{2,1,0:T(8,128)} %broadcast_in_dim.64.req, s32[8,256]{1,0:T(8,128)} %broadcast_in_dim.65.slot, ...), custom_call_target="tpu_custom_call" | custom-call | tf_op jit(solution)/shard_map/step/pallas_call | solution.py:735
  161.8 0.0 copy-done.2
  161.8 0.0 copy-done.5
  161.9 0.0 copy-done.6
  161.9 0.3 conditional.1
  162.2 1.8 %reshape.406 = bf16[64,4,640]{2,1,0:T(4,128)(2,1)} reshape(bf16[256,640]{1,0:T(8,128)(2,1)} %get-tuple-element.57) | data formatting | bytes 655360 | tf_op jit(solution)/shard_map/cond/branch_0_fun/reshape | solution.py:940
  164.0 1.5 copy.155
  165.5 0.6 copy.156
  (15 shorter events, 0.1 us)
Async XLA Ops:
  15.4 146.4 %copy-start.2 = (bf16[40,8192]{1,0:T(8,128)(2,1)S(1)}, bf16[40,8192]{1,0:T(8,128)(2,1)}, u32[]{:S(2)}) copy-start(bf16[40,8192]{1,0:T(8,128)(2,1)} %wq.1) | copy-start | bytes 1966084
  15.4 146.4 %copy-start.5 = (bf16[40,1024]{1,0:T(8,128)(2,1)S(1)}, bf16[40,1024]{1,0:T(8,128)(2,1)}, u32[]{:S(2)}) copy-start(bf16[40,1024]{1,0:T(8,128)(2,1)} %wk.1) | copy-start | bytes 245764
  15.4 146.4 %copy-start.6 = (bf16[40,1024]{1,0:T(8,128)(2,1)S(1)}, bf16[40,1024]{1,0:T(8,128)(2,1)}, u32[]{:S(2)}) copy-start(bf16[40,1024]{1,0:T(8,128)(2,1)} %wv.1) | copy-start | bytes 245764
  15.4 146.4 %copy-start.9 = (s32[64]{0:T(128)S(1)}, s32[64]{0:T(128)}, u32[]{:S(2)}) copy-start(s32[64]{0:T(128)} %lengths.1) | copy-start | bytes 772
  15.5 146.4 %copy-start.10 = (s32[64,4]{0,1:T(4,128)S(1)}, s32[64,4]{0,1:T(4,128)}, u32[]{:S(2)}) copy-start(s32[64,4]{0,1:T(4,128)} %param.16) | copy-start | bytes 3076
  15.5 146.4 %copy-start.11 = (bf16[640]{0:T(1024)(128)(2,1)S(1)}, bf16[640]{0:T(1024)(128)(2,1)}, u32[]{:S(2)}) copy-start(bf16[640]{0:T(1024)(128)(2,1)} %param.19) | copy-start | bytes 3844
  15.5 146.4 %copy-start.12 = (bf16[128]{0:T(256)(128)(2,1)S(1)}, bf16[128]{0:T(256)(128)(2,1)}, u32[]{:S(2)}) copy-start(bf16[128]{0:T(256)(128)(2,1)} %param.24) | copy-start | bytes 772
  15.5 146.4 %copy-start.13 = (bf16[128]{0:T(256)(128)(2,1)S(1)}, bf16[128]{0:T(256)(128)(2,1)}, u32[]{:S(2)}) copy-start(bf16[128]{0:T(256)(128)(2,1)} %param.25) | copy-start | bytes 772
